TPU v7x, 32 devices: a whole 2x2x4 slice. The times are simulated.
32 devices in a mesh: row: 8 (over y, x, core), col: 4 (over z).
Axes of the slice: x: 2, y: 2, z: 4, core: 2. Of those that a mesh axis runs over, the one named last changes fastest.
Arguments:
- alignment_tensor: bfloat16 [128, 256, 256], P(None, ('row', 'col')), may hold values from -6 to 6
- alignment_scaling_vector: float32 [256], replicated, may hold values from 0.1 to 1.9
- first_factor_matrix: bfloat16 [256, 32], replicated, may hold values from -0.375 to 0.375
- second_factor_matrix: bfloat16 [256, 32], replicated, may hold values from -0.375 to 0.375
- final_mapping_matrix: bfloat16 [1024, 128], replicated, may hold values from -2 to 2
- final_offset_vector: float32 [128], replicated, may hold values from -3 to 3
- couple_tensor: bfloat16 [256, 256, 128], P('row', 'col'), may hold values from -6 to 6
- feedforward_scaling_vector: float32 [128], replicated, may hold values from 0.1 to 1.9
- feedforward_expand_matrix: bfloat16 [128, 512], replicated, may hold values from -0.5 to 0.5
- feedforward_contract_matrix: bfloat16 [512, 128], replicated, may hold values from -0.25 to 0.25
- upstream_sensitivity: bfloat16 [256, 256, 128], P('row', 'col'), may hold values from -6 to 6
Outputs:
- couple_revised_tensor: bfloat16 [256, 256, 128], P('row', 'col')
- couple_sensitivity: bfloat16 [256, 256, 128], P('row', 'col')
- alignment_sensitivity: bfloat16 [128, 256, 256], P(None, ('row', 'col'))
- grad_out_proj: float32 [1024, 128], replicated
- grad_trans_in: float32 [128, 512], replicated
- grad_trans_out: float32 [512, 128], replicated
- first_factor_matrix_sensitivity: float32 [256, 32], replicated
- second_factor_matrix_sensitivity: float32 [256, 32], replicated
All inputs are finite; a program needn't handle non-finite values.
Results may differ from a plain program's by a relative error of at most 0.02.
Values may be sent and summed in bfloat16 or wider, within the bound.
A program may use at most 64 MiB of HBM per device.

v0:
```python
import jax
import jax.numpy as jnp
from jax import lax
from jax.sharding import PartitionSpec as P

EPSILON = 1e-05
ROOT_HALF = 0.7071067811865476
INV_ROOT_TWO_PI = 0.3989422804014327


def smooth_gate(values):
    return 0.5 * values * (1.0 + jax.scipy.special.erf(values * ROOT_HALF))


def smooth_slope(values):
    return (
        0.5 * (1.0 + jax.scipy.special.erf(values * ROOT_HALF))
        + values * jnp.exp(-0.5 * values * values) * INV_ROOT_TWO_PI
    )


def standardize_features(values, gain_vec):
    average = jnp.mean(values, axis=-1, keepdims=True)
    centred = values - average
    variance = jnp.mean(centred * centred, axis=-1, keepdims=True)
    inv_scale = lax.rsqrt(variance + EPSILON)
    vhat_values = centred * inv_scale
    return (vhat_values * gain_vec, vhat_values, inv_scale)


def standardize_reverse_mode(incoming, vhat_values, inv_scale, gain_vec):
    scaled = incoming * gain_vec
    return inv_scale * (
        scaled
        - jnp.mean(scaled, axis=-1, keepdims=True)
        - vhat_values * jnp.mean(scaled * vhat_values, axis=-1, keepdims=True)
    )


def on_device(
    alignment_tensor,
    alignment_scaling_vector,
    first_factor_matrix,
    second_factor_matrix,
    final_mapping_matrix,
    final_offset_vector,
    couple_tensor,
    feedforward_scaling_vector,
    feedforward_expand_matrix,
    feedforward_contract_matrix,
    upstream_sensitivity,
):
    aligned_number, shard_extent, alignment_feature_size = alignment_tensor.shape
    channels = first_factor_matrix.shape[1]
    row_count, col_count, pair_width = couple_tensor.shape
    amino_number = row_count * lax.axis_size("row")
    row_at = lax.axis_index("row")
    col_at = lax.axis_index("col")
    rescaled_complete_lines, alignment_centered_scaled, alignment_reciprocal_spread = (
        standardize_features(alignment_tensor.astype(jnp.float32), alignment_scaling_vector)
    )
    rescaled_lines = rescaled_complete_lines.astype(jnp.bfloat16)
    left_local = jnp.einsum(
        "srm,mc->rcs", rescaled_lines, first_factor_matrix, preferred_element_type=jnp.float32
    ).astype(jnp.bfloat16)
    right_local = jnp.einsum(
        "srm,mc->rcs", rescaled_lines, second_factor_matrix, preferred_element_type=jnp.float32
    ).astype(jnp.bfloat16)
    row_ratio = lax.axis_size("row") // lax.axis_size("col")
    left_all, right_all = (
        lax.all_gather(left_local, ("row", "col"), axis=0, tiled=True),
        lax.all_gather(right_local, ("row", "col"), axis=0, tiled=True),
    )
    left_rows = lax.dynamic_slice_in_dim(left_all, row_at * row_count, row_count, 0)
    right_cols = lax.dynamic_slice_in_dim(right_all, col_at * col_count, col_count, 0)
    block_rows = 8

    def block_step(totals, start_row):
        acc_right, summed_result_state, summed_entry_state, summed_feedforward_result = totals
        left_block = lax.dynamic_slice_in_dim(left_rows, start_row, block_rows, 0)
        outer_prod = (
            jnp.einsum("ics,jes->ijce", left_block, right_cols, preferred_element_type=jnp.float32)
            / aligned_number
        ).astype(jnp.bfloat16)
        outer_prod = outer_prod.reshape(block_rows * col_count, channels * channels)
        pair_block = lax.dynamic_slice_in_dim(couple_tensor, start_row, block_rows, 0).reshape(
            -1, pair_width
        )
        cot_block = lax.dynamic_slice_in_dim(
            upstream_sensitivity, start_row, block_rows, 0
        ).reshape(-1, pair_width)
        update = (
            jnp.dot(outer_prod, final_mapping_matrix, preferred_element_type=jnp.float32)
            + final_offset_vector
        )
        middle = (pair_block.astype(jnp.float32) + update).astype(jnp.bfloat16)
        middle_full = middle.astype(jnp.float32)
        normed_pair_full, pair_hat, pair_inv = standardize_features(
            middle_full, feedforward_scaling_vector
        )
        normed_pair = normed_pair_full.astype(jnp.bfloat16)
        pre_gate = jnp.dot(
            normed_pair, feedforward_expand_matrix, preferred_element_type=jnp.float32
        )
        hidden = smooth_gate(pre_gate).astype(jnp.bfloat16)
        result = (
            middle_full
            + jnp.dot(hidden, feedforward_contract_matrix, preferred_element_type=jnp.float32)
        ).astype(jnp.bfloat16)
        summed_feedforward_result = summed_feedforward_result + jnp.einsum(
            "pk,pn->kn", hidden, cot_block, preferred_element_type=jnp.float32
        )
        hidden_grad = (
            jnp.dot(cot_block, feedforward_contract_matrix.T, preferred_element_type=jnp.float32)
            * smooth_slope(pre_gate)
        ).astype(jnp.bfloat16)
        summed_entry_state = summed_entry_state + jnp.einsum(
            "pk,pn->kn", normed_pair, hidden_grad, preferred_element_type=jnp.float32
        )
        norm_grad = jnp.dot(
            hidden_grad, feedforward_expand_matrix.T, preferred_element_type=jnp.float32
        )
        grad_block = (
            cot_block.astype(jnp.float32)
            + standardize_reverse_mode(norm_grad, pair_hat, pair_inv, feedforward_scaling_vector)
        ).astype(jnp.bfloat16)
        summed_result_state = summed_result_state + jnp.einsum(
            "pk,pn->kn", outer_prod, grad_block, preferred_element_type=jnp.float32
        )
        outer_grad = jnp.dot(
            grad_block, final_mapping_matrix.T, preferred_element_type=jnp.float32
        ).astype(jnp.bfloat16)
        outer_grad = outer_grad.reshape(block_rows, col_count, channels, channels)
        left_part = (
            jnp.einsum("ijce,jes->ics", outer_grad, right_cols, preferred_element_type=jnp.float32)
            / aligned_number
        )
        acc_right = (
            acc_right
            + jnp.einsum(
                "ijce,ics->jes", outer_grad, left_block, preferred_element_type=jnp.float32
            )
            / aligned_number
        )
        return (
            (acc_right, summed_result_state, summed_entry_state, summed_feedforward_result),
            (result, grad_block, left_part),
        )

    initial = (
        jnp.zeros((col_count, channels, aligned_number), jnp.float32),
        jnp.zeros((channels * channels, pair_width), jnp.float32),
        jnp.zeros(feedforward_expand_matrix.shape, jnp.float32),
        jnp.zeros(feedforward_contract_matrix.shape, jnp.float32),
    )
    starts = jnp.arange(row_count // block_rows, dtype=jnp.int32) * block_rows
    totals, stacked = lax.scan(block_step, initial, starts)
    acc_right, summed_result_state, summed_entry_state, summed_feedforward_result = totals
    results, grad_blocks, left_parts = stacked
    couple_revised_tensor = results.reshape(row_count, col_count, pair_width)
    couple_sensitivity = grad_blocks.reshape(row_count, col_count, pair_width)
    left_parts = left_parts.reshape(row_count, channels, aligned_number)
    left_grad = lax.psum_scatter(
        left_parts.astype(jnp.bfloat16), "col", scatter_dimension=0, tiled=True
    )
    col_total = lax.axis_size("col")
    grouped = acc_right.reshape(row_ratio, col_total, shard_extent * channels, aligned_number)
    routed = lax.all_to_all(
        grouped.astype(jnp.bfloat16), "col", split_axis=1, concat_axis=0, tiled=True
    ).astype(grouped.dtype)
    routed = routed.reshape(row_ratio * col_total * shard_extent, channels, aligned_number)
    right_grad = lax.psum_scatter(
        routed.astype(jnp.bfloat16), "row", scatter_dimension=0, tiled=True
    )
    left_weight = jnp.einsum(
        "srm,rcs->mc", rescaled_lines, left_grad, preferred_element_type=jnp.float32
    )
    right_weight = jnp.einsum(
        "srm,rcs->mc", rescaled_lines, right_grad, preferred_element_type=jnp.float32
    )
    rescaled_sensitivity = jnp.einsum(
        "rcs,mc->srm", left_grad, first_factor_matrix, preferred_element_type=jnp.float32
    )
    rescaled_sensitivity = rescaled_sensitivity + jnp.einsum(
        "rcs,mc->srm", right_grad, second_factor_matrix, preferred_element_type=jnp.float32
    )
    alignment_sensitivity = standardize_reverse_mode(
        rescaled_sensitivity,
        alignment_centered_scaled,
        alignment_reciprocal_spread,
        alignment_scaling_vector,
    ).astype(jnp.bfloat16)
    summed = lax.psum(
        (
            summed_result_state,
            summed_entry_state,
            summed_feedforward_result,
            left_weight,
            right_weight,
        ),
        ("row", "col"),
    )
    return (
        couple_revised_tensor,
        couple_sensitivity,
        alignment_sensitivity,
        summed[0] / amino_number,
        summed[1] / amino_number,
        summed[2] / amino_number,
        summed[3] / amino_number,
        summed[4] / amino_number,
    )


def solution(mesh):
    return jax.shard_map(
        on_device,
        mesh=mesh,
        in_specs=(
            P(None, ("row", "col"), None),
            P(),
            P(),
            P(),
            P(),
            P(),
            P("row", "col", None),
            P(),
            P(),
            P(),
            P("row", "col", None),
        ),
        out_specs=(
            P("row", "col", None),
            P("row", "col", None),
            P(None, ("row", "col"), None),
            P(),
            P(),
            P(),
            P(),
            P(),
        ),
        check_vma=False,
    )
```

profile of v0, /device:TPU:0, one launch (start us, length us, event | category | flops | bytes accessed | tf_op | source)
XLA Modules:
  0.0 593.1 jit_solution(2118915596024095089)
XLA Ops:
  7.3 1.3 convert_reduce_fusion
  8.6 1.4 fusion.50
  10.0 2.1 fusion.44
  13.5 58.0 %all-gather.5.cloned.1.call-done = bf16[256,32,128]{2,1,0:T(8,128)(2,1)} async-done(((bf16[8,32,128]{2,1,0:T(8,128)(2,1)}), bf16[256,32,128]{2,1,0:T(8,128)(2,1)}) %all-gather.5.cloned.1.call-update) | async-done | bytes 2097168 | tf_op jit(solution)/shard_map/all_gather | solution.py:72
  72.8 57.6 %all-gather.3.cloned.1.call-done = bf16[256,32,128]{2,1,0:T(8,128)(2,1)} async-done(((bf16[8,32,128]{2,1,0:T(8,128)(2,1)}), bf16[256,32,128]{2,1,0:T(8,128)(2,1)}) %all-gather.3.cloned.1.call-update) | async-done | bytes 2097168 | tf_op jit(solution)/shard_map/all_gather | solution.py:71
  131.4 137.0 %while.23 = (s32[]{:T(128)}, f32[64,32,128]{2,1,0:T(8,128)}, f32[1024,128]{1,0:T(8,128)}, f32[128,512]{1,0:T(8,128)}, f32[512,128]{1,0:T(8,128)}, /*index=5*/bf1...) while((s32[]{:T(128)}, f32[64,32,128]{2,1,0:T(8,128)}, ...), condition=%wide.region_7.8_spmd.clone, body=%wide.region_2.7_spmd.clone.sunk | while | flops 1217036800 | bytes 64803780 | solution.py:157
  137.8 1.4 copy.105
  139.2 1.3 reshape.103
  140.5 1.4 fusion.136
  148.8 1.1 reshape.104
  149.9 3.4 fusion.141
  153.3 7.3 %copy.108 = bf16[8,64,32,32]{2,3,0,1:T(8,128)(2,1)} copy(bf16[8,64,32,32]{1,0,3,2:T(8,128)(2,1)S(1)} %reshape.104) | data formatting | bytes 2097152 | tf_op jit(solution)/shard_map/while/body/eval_jaxpr/reshape | solution.py:133
  160.6 3.3 fusion.139
  171.4 1.4 copy.105
  172.7 1.3 reshape.103
  174.0 1.4 fusion.136
  178.5 1.9 convolution_add_fusion.10
  184.4 3.4 fusion.141
  187.8 7.3 %copy.108 = bf16[8,64,32,32]{2,3,0,1:T(8,128)(2,1)} copy(bf16[8,64,32,32]{1,0,3,2:T(8,128)(2,1)S(1)} %reshape.104) | data formatting | bytes 2097152 | tf_op jit(solution)/shard_map/while/body/eval_jaxpr/reshape | solution.py:133
  195.1 3.3 fusion.139
  205.9 1.4 copy.105
  207.2 1.3 reshape.103
  208.5 1.4 fusion.136
  212.9 1.9 convolution_add_fusion.10
  218.9 3.4 fusion.141
  222.2 7.3 %copy.108 = bf16[8,64,32,32]{2,3,0,1:T(8,128)(2,1)} copy(bf16[8,64,32,32]{1,0,3,2:T(8,128)(2,1)S(1)} %reshape.104) | data formatting | bytes 2097152 | tf_op jit(solution)/shard_map/while/body/eval_jaxpr/reshape | solution.py:133
  229.6 3.3 fusion.139
  240.3 1.4 copy.105
  241.7 1.3 reshape.103
  243.0 1.4 fusion.136
  247.4 1.9 convolution_add_fusion.10
  253.4 3.4 fusion.141
  256.7 7.3 %copy.108 = bf16[8,64,32,32]{2,3,0,1:T(8,128)(2,1)} copy(bf16[8,64,32,32]{1,0,3,2:T(8,128)(2,1)S(1)} %reshape.104) | data formatting | bytes 2097152 | tf_op jit(solution)/shard_map/while/body/eval_jaxpr/reshape | solution.py:133
  264.1 3.3 fusion.139
  268.4 1.3 convert_element_type.85
  270.6 3.8 all-to-all-start
  275.0 127.8 %all-reduce.7.cloned.1.call-done = (f32[1024,128]{1,0:T(8,128)}, f32[128,512]{1,0:T(8,128)}, f32[512,128]{1,0:T(8,128)}) async-done(((f32[1024,128]{1,0:T(8,128)}, f32[128,512]{1,0:T(8,128)}, f32[512,128]{1,0:T(8,128)}), (f32[1024,128]{1,0:T(8,128)}, f32[128,512]{1,0:T(8,128)}, f32[512,128]{1,0:T(8,128)})) %all-reduce.7.cloned.1.call-update) | async-done | bytes 1048592 | tf_op jit(solution)/shard_map/psum | solution.py:193
  402.8 1.7 broadcast_multiply_fusion.5
  405.4 1.7 broadcast_multiply_fusion.4
  407.0 1.9 broadcast_multiply_fusion.3
  408.9 14.9 %reduce-scatter.3.cloned.1.call-done = bf16[8,32,128]{2,1,0:T(8,128)(2,1)} async-done(((bf16[32,32,128]{2,1,0:T(8,128)(2,1)}), bf16[8,32,128]{2,1,0:T(8,128)(2,1)}) %reduce-scatter.3.cloned.1.call-update) | async-done | bytes 65552 | tf_op jit(solution)/shard_map/reduce_scatter | solution.py:163
  423.8 1.9 convolution_bitcast_fusion.2
  425.7 1.2 fusion.53
  426.9 32.7 %reduce-scatter.5.cloned.1.call-done = bf16[8,32,128]{2,1,0:T(8,128)(2,1)} async-done(((bf16[64,32,128]{2,1,0:T(8,128)(2,1)}), bf16[8,32,128]{2,1,0:T(8,128)(2,1)}) %reduce-scatter.5.cloned.1.call-update) | async-done | bytes 65552 | tf_op jit(solution)/shard_map/reduce_scatter | solution.py:172
  459.6 1.9 convolution_bitcast_fusion.1
  461.6 1.8 fusion.61
  465.2 119.7 %all-reduce.5.cloned.1.call-done = (f32[256,32]{0,1:T(8,128)}, f32[256,32]{0,1:T(8,128)}) async-done(((f32[256,32]{0,1:T(8,128)}, f32[256,32]{0,1:T(8,128)}), (f32[256,32]{0,1:T(8,128)}, f32[256,32]{0,1:T(8,128)})) %all-reduce.5.cloned.1.call-update) | async-done | bytes 65552 | tf_op jit(solution)/shard_map/psum | solution.py:193
  584.9 1.4 broadcast_multiply_fusion.6
  (315 shorter events, 56.1 us)
Async XLA Ops:
  7.2 5.1 copy-start.12
  7.2 5.1 copy-start.28
  7.2 5.1 copy-start.26
  7.2 64.3 %all-gather.5.cloned.1.call-start = ((), (), s32[]{:S(2)}) async-start(), calls=%async_computation.4 | async-start | bytes 2162688 | tf_op jit(solution)/shard_map/all_gather | solution.py:72
  8.6 63.0 %copy-start.22 = (f32[128,8]{0,1:T(8,128)}, f32[128,8]{0,1:T(8,128)S(1)}, u32[]{:S(2)}) copy-start(f32[128,8]{0,1:T(8,128)S(1)} %broadcast_multiply_fusion.10) | copy-start | bytes 12292
  10.0 61.5 %copy-start.24 = (f32[128,8]{0,1:T(8,128)}, f32[128,8]{0,1:T(8,128)S(1)}, u32[]{:S(2)}) copy-start(f32[128,8]{0,1:T(8,128)S(1)} %add_rsqrt_fusion.1) | copy-start | bytes 12292
  12.2 118.2 %all-gather.3.cloned.1.call-start = ((), (), s32[]{:S(2)}) async-start(), calls=%async_computation.3 | async-start | bytes 2162688 | tf_op jit(solution)/shard_map/all_gather | solution.py:71
  13.4 389.4 %all-reduce.7.cloned.1.call-start = ((), (), s32[]{:S(2)}) async-start(), calls=%async_computation.8 | async-start | bytes 2097152 | tf_op jit(solution)/shard_map/psum | solution.py:193
  131.4 2.9 copy-start.30
  131.4 6.4 %copy-start.6 = (bf16[64,32,128]{2,0,1:T(8,128)(2,1)}, bf16[64,32,128]{2,0,1:T(8,128)(2,1)S(1)}, u32[]{:S(2)}) copy-start(bf16[64,32,128]{2,0,1:T(8,128)(2,1)S(1)} %get-tuple-element.512) | copy-start | bytes 1572868 | tf_op jit(solution)/shard_map/while
  131.4 6.4 %copy-start.15 = (bf16[32,32,128]{2,1,0:T(8,128)(2,1)}, bf16[32,32,128]{2,1,0:T(8,128)(2,1)S(1)}, u32[]{:S(2)}) copy-start(bf16[32,32,128]{2,1,0:T(8,128)(2,1)S(1)} %get-tuple-element.511) | copy-start | bytes 786436 | tf_op jit(solution)/shard_map/while
  153.2 7.4 %copy-start.19 = (bf16[4,8,32,128]{3,2,1,0:T(8,128)(2,1)}, bf16[4,8,32,128]{3,2,1,0:T(8,128)(2,1)S(1)}, u32[]{:S(2)}) copy-start(bf16[4,8,32,128]{3,2,1,0:T(8,128)(2,1)S(1)} %fusion.141) | copy-start | bytes 786436 | tf_op jit(solution)/shard_map/while
  153.3 7.3 %copy-start.1 = (f32[64,32,128]{2,1,0:T(8,128)S(1)}, f32[64,32,128]{2,1,0:T(8,128)}, u32[]{:S(2)}) copy-start(f32[64,32,128]{2,1,0:T(8,128)} %get-tuple-element.480) | copy-start | bytes 3145732 | tf_op jit(solution)/shard_map/while
  160.6 4.3 copy-start.7
  160.6 4.3 copy-start.16
  160.6 4.3 copy-start.31
  164.9 2.9 copy-start.30
  164.9 6.4 %copy-start.6 = (bf16[64,32,128]{2,0,1:T(8,128)(2,1)}, bf16[64,32,128]{2,0,1:T(8,128)(2,1)S(1)}, u32[]{:S(2)}) copy-start(bf16[64,32,128]{2,0,1:T(8,128)(2,1)S(1)} %get-tuple-element.512) | copy-start | bytes 1572868 | tf_op jit(solution)/shard_map/while
  165.0 6.4 %copy-start.15 = (bf16[32,32,128]{2,1,0:T(8,128)(2,1)}, bf16[32,32,128]{2,1,0:T(8,128)(2,1)S(1)}, u32[]{:S(2)}) copy-start(bf16[32,32,128]{2,1,0:T(8,128)(2,1)S(1)} %get-tuple-element.511) | copy-start | bytes 786436 | tf_op jit(solution)/shard_map/while
  187.7 7.4 %copy-start.19 = (bf16[4,8,32,128]{3,2,1,0:T(8,128)(2,1)}, bf16[4,8,32,128]{3,2,1,0:T(8,128)(2,1)S(1)}, u32[]{:S(2)}) copy-start(bf16[4,8,32,128]{3,2,1,0:T(8,128)(2,1)S(1)} %fusion.141) | copy-start | bytes 786436 | tf_op jit(solution)/shard_map/while
  187.7 7.3 %copy-start.1 = (f32[64,32,128]{2,1,0:T(8,128)S(1)}, f32[64,32,128]{2,1,0:T(8,128)}, u32[]{:S(2)}) copy-start(f32[64,32,128]{2,1,0:T(8,128)} %get-tuple-element.480) | copy-start | bytes 3145732 | tf_op jit(solution)/shard_map/while
  195.1 4.3 copy-start.7
  195.1 4.3 copy-start.16
  195.1 4.3 copy-start.31
  199.4 2.9 copy-start.30
  199.4 6.4 %copy-start.6 = (bf16[64,32,128]{2,0,1:T(8,128)(2,1)}, bf16[64,32,128]{2,0,1:T(8,128)(2,1)S(1)}, u32[]{:S(2)}) copy-start(bf16[64,32,128]{2,0,1:T(8,128)(2,1)S(1)} %get-tuple-element.512) | copy-start | bytes 1572868 | tf_op jit(solution)/shard_map/while
  199.5 6.4 %copy-start.15 = (bf16[32,32,128]{2,1,0:T(8,128)(2,1)}, bf16[32,32,128]{2,1,0:T(8,128)(2,1)S(1)}, u32[]{:S(2)}) copy-start(bf16[32,32,128]{2,1,0:T(8,128)(2,1)S(1)} %get-tuple-element.511) | copy-start | bytes 786436 | tf_op jit(solution)/shard_map/while
  222.2 7.4 %copy-start.19 = (bf16[4,8,32,128]{3,2,1,0:T(8,128)(2,1)}, bf16[4,8,32,128]{3,2,1,0:T(8,128)(2,1)S(1)}, u32[]{:S(2)}) copy-start(bf16[4,8,32,128]{3,2,1,0:T(8,128)(2,1)S(1)} %fusion.141) | copy-start | bytes 786436 | tf_op jit(solution)/shard_map/while
  222.2 7.3 %copy-start.1 = (f32[64,32,128]{2,1,0:T(8,128)S(1)}, f32[64,32,128]{2,1,0:T(8,128)}, u32[]{:S(2)}) copy-start(f32[64,32,128]{2,1,0:T(8,128)} %get-tuple-element.480) | copy-start | bytes 3145732 | tf_op jit(solution)/shard_map/while
  229.6 4.3 copy-start.7
  229.6 4.3 copy-start.16
  229.6 4.3 copy-start.31
  233.9 6.4 %copy-start.6 = (bf16[64,32,128]{2,0,1:T(8,128)(2,1)}, bf16[64,32,128]{2,0,1:T(8,128)(2,1)S(1)}, u32[]{:S(2)}) copy-start(bf16[64,32,128]{2,0,1:T(8,128)(2,1)S(1)} %get-tuple-element.512) | copy-start | bytes 1572868 | tf_op jit(solution)/shard_map/while
  233.9 6.4 %copy-start.15 = (bf16[32,32,128]{2,1,0:T(8,128)(2,1)}, bf16[32,32,128]{2,1,0:T(8,128)(2,1)S(1)}, u32[]{:S(2)}) copy-start(bf16[32,32,128]{2,1,0:T(8,128)(2,1)S(1)} %get-tuple-element.511) | copy-start | bytes 786436 | tf_op jit(solution)/shard_map/while
  256.7 7.4 %copy-start.19 = (bf16[4,8,32,128]{3,2,1,0:T(8,128)(2,1)}, bf16[4,8,32,128]{3,2,1,0:T(8,128)(2,1)S(1)}, u32[]{:S(2)}) copy-start(bf16[4,8,32,128]{3,2,1,0:T(8,128)(2,1)S(1)} %fusion.141) | copy-start | bytes 786436 | tf_op jit(solution)/shard_map/while
  256.7 7.3 %copy-start.1 = (f32[64,32,128]{2,1,0:T(8,128)S(1)}, f32[64,32,128]{2,1,0:T(8,128)}, u32[]{:S(2)}) copy-start(f32[64,32,128]{2,1,0:T(8,128)} %get-tuple-element.480) | copy-start | bytes 3145732 | tf_op jit(solution)/shard_map/while
  264.1 4.3 copy-start.7
  264.1 4.3 copy-start.16
  264.1 4.3 copy-start.31
  270.6 153.2 %copy-start.13 = (bf16[128,8,256]{2,1,0:T(8,128)(2,1)S(1)}, bf16[128,8,256]{2,1,0:T(8,128)(2,1)}, u32[]{:S(2)}) copy-start(bf16[128,8,256]{2,1,0:T(8,128)(2,1)} %param.13) | copy-start | bytes 1572868
  270.6 153.2 %copy-start.23 = (f32[128,8]{0,1:T(8,128)S(1)}, f32[128,8]{0,1:T(8,128)}, u32[]{:S(2)}) copy-start(f32[128,8]{0,1:T(8,128)} %copy-done.22) | copy-start | bytes 12292
  270.6 153.2 %copy-start.25 = (f32[128,8]{0,1:T(8,128)S(1)}, f32[128,8]{0,1:T(8,128)}, u32[]{:S(2)}) copy-start(f32[128,8]{0,1:T(8,128)} %copy-done.24) | copy-start | bytes 12292
  270.6 153.2 %copy-start.29 = (f32[256]{0:T(256)S(1)}, f32[256]{0:T(256)}, u32[]{:S(2)}) copy-start(f32[256]{0:T(256)} %param.14) | copy-start | bytes 3076
  270.6 133.9 %all-to-all-start = ((bf16[2,4,256,128]{3,2,0,1:T(8,128)(2,1)}), bf16[2,4,256,128]{3,2,0,1:T(8,128)(2,1)S(1)}, u32[]{:S(2)}, u32[]{:S(2)}) async-start(bf16[2,4,256,128]{3,2,0,1:T(8,128)(2,1)} %copy.66), calls=%async_computation.1 | async-start | bytes 1048576 | tf_op jit(solution)/shard_map/all_to_all | solution.py:168
  274.4 149.4 %reduce-scatter.3.cloned.1.call-start = ((), (), s32[]{:S(2)}) async-start(), calls=%async_computation.5 | async-start | bytes 327680 | tf_op jit(solution)/shard_map/reduce_scatter | solution.py:163
  274.5 151.3 %copy-start.27 = (bf16[256,32]{0,1:T(8,128)(2,1)S(1)}, bf16[256,32]{0,1:T(8,128)(2,1)}, u32[]{:S(2)}) copy-start(bf16[256,32]{0,1:T(8,128)(2,1)} %param.15) | copy-start | bytes 49156
  275.0 184.6 %reduce-scatter.5.cloned.1.call-start = ((), (), s32[]{:S(2)}) async-start(), calls=%async_computation.6 | async-start | bytes 589824 | tf_op jit(solution)/shard_map/reduce_scatter | solution.py:172
  405.3 179.6 %all-reduce.5.cloned.1.call-start = ((), (), s32[]{:S(2)}) async-start(), calls=%async_computation.7 | async-start | bytes 131072 | tf_op jit(solution)/shard_map/psum | solution.py:193
  (51 other events, 77.8 us)
Sparse Core Ops, SparseCore 0:
  12.3 59.1 all-gather.4
  75.0 55.3 all-gather.2
  268.6 134.1 all-reduce.6
  405.0 18.7 reduce-scatter.2
  427.3 32.2 reduce-scatter.4
  466.7 118.1 all-reduce.4
where the time goes:
time: 596 us; the launch traced here: 593 us
  waiting for transfers between devices  411 us (69%)
  local copies, waits for them, and re-layouts  78.1 us (13%)
  matrix products  63.4 us (11%)
  between operations  14.4 us (2%)
  other arithmetic  12.2 us (2%)
  loops' own time  9.79 us (2%)
    psum x2, waiting for transfers between devices, on_device(): lax.psum((summed_result_state, summed_entry_state, summed_feedforward_res...  247 us
    all_gather x1, waiting for transfers between devices, on_device(): lax.all_gather(right_local, ('row', 'col'), axis=0, tiled=True)  58 us
    all_gather x1, waiting for transfers between devices, on_device(): lax.all_gather(left_local, ('row', 'col'), axis=0, tiled=True)  57.6 us
    reshape x8, local copies, waits for them, and re-layouts, block_step(): outer_grad = outer_grad.reshape(block_rows, col_count, channels, channels)  33.7 us
    reduce_scatter x1, waiting for transfers between devices, on_device(): lax.psum_scatter(routed.astype(jnp.bfloat16), 'row', scatter_dimension=0,...  32.7 us
    reduce_scatter x1, waiting for transfers between devices, on_device(): lax.psum_scatter(left_parts.astype(jnp.bfloat16), 'col', scatter_dimensio...  14.9 us
    dot_general x4, matrix products, block_step(): jnp.einsum('ijce,jes->ics', outer_grad, right_cols, preferred_element_typ...  13.4 us
    dot_general x4, matrix products, block_step(): jnp.einsum('ijce,ics->jes', outer_grad, left_block, preferred_element_typ...  13.2 us
  transfers between devices with their start and end apart: 7, of which 6 were waited for; matrix products, arithmetic and copies ran while one was open for 3% of the time, Pallas kernels for 0%

commit v1 on v0

v1 whole, which is shorter than its diff:
```python
import functools

import jax
import jax.numpy as jnp
from jax import lax
from jax.experimental import pallas as pl
from jax.experimental.pallas import tpu as pltpu
from jax.sharding import PartitionSpec as P

EPSILON = 1e-05
ROOT_HALF = 0.7071067811865476
INV_ROOT_TWO_PI = 0.3989422804014327
F32 = jnp.float32
BF16 = jnp.bfloat16
MESH = pl.DeviceIdType.MESH
VM = pl.BlockSpec(memory_space=pltpu.VMEM)
LANES = 128


def standardize_features(values, gain_vec):
    average = jnp.mean(values, axis=-1, keepdims=True)
    centred = values - average
    variance = jnp.mean(centred * centred, axis=-1, keepdims=True)
    inv_scale = lax.rsqrt(variance + EPSILON)
    vhat_values = centred * inv_scale
    return (vhat_values * gain_vec, vhat_values, inv_scale)


def standardize_reverse_mode(incoming, vhat_values, inv_scale, gain_vec):
    scaled = incoming * gain_vec
    return inv_scale * (
        scaled
        - jnp.mean(scaled, axis=-1, keepdims=True)
        - vhat_values * jnp.mean(scaled * vhat_values, axis=-1, keepdims=True)
    )


def positions(rows, cols):
    r = lax.axis_index("row")
    z = lax.axis_index("col")
    here = r * cols + z
    there = z * rows + r
    return r, z, here, there


def greet(rows, cols, r, z, partners=(), apart=None):
    barrier = pltpu.get_barrier_semaphore()
    for k in range(1, rows):
        pl.semaphore_signal(
            barrier, inc=1, device_id=(lax.rem(r + k, rows), z), device_id_type=MESH
        )
    for k in range(1, cols):
        pl.semaphore_signal(
            barrier, inc=1, device_id=(r, lax.rem(z + k, cols)), device_id_type=MESH
        )
    if partners:

        @pl.when(apart)
        def _():
            for partner in partners:
                pl.semaphore_signal(barrier, inc=1, device_id=partner, device_id_type=MESH)

    expected = rows - 1 + cols - 1
    if partners:
        expected = expected + len(partners) * apart.astype(jnp.int32)
    pl.semaphore_wait(barrier, expected)


def send(src, dst, send_sem, recv_sem, device):
    return pltpu.make_async_remote_copy(
        src_ref=src,
        dst_ref=dst,
        send_sem=send_sem,
        recv_sem=recv_sem,
        device_id=device,
        device_id_type=MESH,
    )


def gather_kernel(
    rows, cols, left_ref, right_ref, left_out, right_out,
    own_sem, hop_send, hop_recv, left_send, left_recv, right_send, right_recv,
):
    r, z, here, there = positions(rows, cols)
    apart = here != there
    to = (lax.rem(here, rows), here // rows)
    source = (there // cols, lax.rem(there, cols))
    greet(rows, cols, r, z, (to, source), apart)

    hop = send(right_ref, right_out.at[to[0]], hop_send, hop_recv, to)
    stay = pltpu.make_async_copy(right_ref, right_out.at[r], hop_send)

    @pl.when(apart)
    def _():
        hop.start()

    @pl.when(jnp.logical_not(apart))
    def _():
        stay.start()

    own = pltpu.make_async_copy(left_ref, left_out.at[z], own_sem)
    own.start()
    lefts = []
    for k in range(1, cols):
        copy = send(
            left_ref, left_out.at[z], left_send.at[k], left_recv.at[k],
            (r, lax.rem(z + k, cols)),
        )
        copy.start()
        lefts.append(copy)

    @pl.when(apart)
    def _():
        send(right_ref, right_out.at[r], hop_send, hop_recv, to).wait_recv()

    @pl.when(jnp.logical_not(apart))
    def _():
        stay.wait()

    rights = []
    for k in range(1, rows):
        copy = send(
            right_out.at[r], right_out.at[r], right_send.at[k], right_recv.at[k],
            (lax.rem(r + k, rows), z),
        )
        copy.start()
        rights.append(copy)
    own.wait()

    @pl.when(apart)
    def _():
        hop.wait_send()

    for k, copy in enumerate(lefts, 1):
        copy.wait_send()
        origin = lax.rem(z - k + cols, cols)
        send(left_ref, left_out.at[origin], left_send.at[k], left_recv.at[k], (r, origin)).wait_recv()
    for k, copy in enumerate(rights, 1):
        copy.wait_send()
        origin = lax.rem(r - k + rows, rows)
        send(
            right_out.at[r], right_out.at[origin], right_send.at[k], right_recv.at[k], (origin, z)
        ).wait_recv()


def gather_sides(rows, cols, left, right):
    return pl.pallas_call(
        functools.partial(gather_kernel, rows, cols),
        out_shape=(
            jax.ShapeDtypeStruct((cols,) + left.shape, left.dtype),
            jax.ShapeDtypeStruct((rows,) + right.shape, right.dtype),
        ),
        in_specs=[VM, VM],
        out_specs=(VM, VM),
        scratch_shapes=[
            pltpu.SemaphoreType.DMA(()),
            pltpu.SemaphoreType.DMA(()),
            pltpu.SemaphoreType.DMA(()),
            pltpu.SemaphoreType.DMA((cols,)),
            pltpu.SemaphoreType.DMA((cols,)),
            pltpu.SemaphoreType.DMA((rows,)),
            pltpu.SemaphoreType.DMA((rows,)),
        ],
        compiler_params=pltpu.CompilerParams(
            collective_id=0, has_side_effects=True, vmem_limit_bytes=24 << 20
        ),
    )(left, right)


def scatter_kernel(
    rows, cols, left_ref, right_ref, weight_ref, left_out, right_out, weight_out,
    right_got, weight_got, right_sum,
    own_sem, hop_send, hop_recv, left_send, left_recv, right_send, right_recv,
    weight_send, weight_recv,
):
    r, z, here, there = positions(rows, cols)
    apart = here != there
    to = (there // cols, lax.rem(there, cols))
    source = (lax.rem(here, rows), here // rows)
    greet(rows, cols, r, z, (to, source), apart)

    started = []
    for k in range(1, rows):
        peer = lax.rem(r + k, rows)
        copy = send(
            right_ref.at[peer], right_got.at[r], right_send.at[k], right_recv.at[k], (peer, z)
        )
        copy.start()
        started.append(copy)
    for k in range(1, cols):
        peer = lax.rem(z + k, cols)
        copy = send(
            left_ref.at[peer], left_out.at[z], left_send.at[k], left_recv.at[k], (r, peer)
        )
        copy.start()
        started.append(copy)
    for k in range(1, rows):
        peer = lax.rem(r + k, rows)
        copy = send(
            weight_ref.at[peer], weight_got.at[r], weight_send.at[k], weight_recv.at[k], (peer, z)
        )
        copy.start()
        started.append(copy)
    own = pltpu.make_async_copy(left_ref.at[z], left_out.at[z], own_sem)
    own.start()

    for k in range(1, rows):
        origin = lax.rem(r - k + rows, rows)
        send(
            right_ref.at[r], right_got.at[origin], right_send.at[k], right_recv.at[k], (origin, z)
        ).wait_recv()
    total = right_ref[r].astype(F32)
    for k in range(1, rows):
        total = total + right_got[lax.rem(r - k + rows, rows)].astype(F32)
    right_sum[...] = total.astype(BF16)

    hop = send(right_sum, right_out, hop_send, hop_recv, to)
    stay = pltpu.make_async_copy(right_sum, right_out, hop_send)

    @pl.when(apart)
    def _():
        hop.start()

    @pl.when(jnp.logical_not(apart))
    def _():
        stay.start()

    for k in range(1, rows):
        origin = lax.rem(r - k + rows, rows)
        send(
            weight_ref.at[r], weight_got.at[origin], weight_send.at[k], weight_recv.at[k],
            (origin, z),
        ).wait_recv()
    total = weight_ref[r].astype(F32)
    for k in range(1, rows):
        total = total + weight_got[lax.rem(r - k + rows, rows)].astype(F32)
    weight_out[...] = total.astype(BF16)

    own.wait()
    for k in range(1, cols):
        origin = lax.rem(z - k + cols, cols)
        send(
            left_ref.at[z], left_out.at[origin], left_send.at[k], left_recv.at[k], (r, origin)
        ).wait_recv()

    @pl.when(apart)
    def _():
        hop.wait()

    @pl.when(jnp.logical_not(apart))
    def _():
        stay.wait()

    for copy in started:
        copy.wait_send()


def scatter_grads(rows, cols, left, right, weight):
    return pl.pallas_call(
        functools.partial(scatter_kernel, rows, cols),
        out_shape=(
            jax.ShapeDtypeStruct(left.shape, left.dtype),
            jax.ShapeDtypeStruct(right.shape[1:], right.dtype),
            jax.ShapeDtypeStruct(weight.shape[1:], weight.dtype),
        ),
        in_specs=[VM] * 3,
        out_specs=(VM,) * 3,
        scratch_shapes=[
            pltpu.VMEM(right.shape, right.dtype),
            pltpu.VMEM(weight.shape, weight.dtype),
            pltpu.VMEM(right.shape[1:], right.dtype),
            pltpu.SemaphoreType.DMA(()),
            pltpu.SemaphoreType.DMA(()),
            pltpu.SemaphoreType.DMA(()),
            pltpu.SemaphoreType.DMA((cols,)),
            pltpu.SemaphoreType.DMA((cols,)),
            pltpu.SemaphoreType.DMA((rows,)),
            pltpu.SemaphoreType.DMA((rows,)),
            pltpu.SemaphoreType.DMA((rows,)),
            pltpu.SemaphoreType.DMA((rows,)),
        ],
        compiler_params=pltpu.CompilerParams(
            collective_id=1, has_side_effects=True, vmem_limit_bytes=24 << 20
        ),
    )(left, right, weight)


def total_kernel(
    rows, cols, big_ref, small_ref, big_out, small_out,
    big_got, small_got, small_col,
    big_send, big_recv, small_send, small_recv,
    bigc_send, bigc_recv, smallc_send, smallc_recv,
    bigr_send, bigr_recv, smallr_send, smallr_recv,
):
    r, z, _, _ = positions(rows, cols)
    greet(rows, cols, r, z)
    started = []

    def go(src, dst, sends, recvs, k, device):
        copy = send(src, dst, sends.at[k], recvs.at[k], device)
        copy.start()
        started.append(copy)

    def arrive(src, dst, sends, recvs, k, device):
        send(src, dst, sends.at[k], recvs.at[k], device).wait_recv()

    for k in range(1, rows):
        peer = lax.rem(r + k, rows)
        go(small_ref.at[peer], small_got.at[r], small_send, small_recv, k, (peer, z))
    for k in range(1, cols):
        peer = lax.rem(z + k, cols)
        go(big_ref.at[peer], big_got.at[z], big_send, big_recv, k, (r, peer))

    total = big_ref[z].astype(F32)
    for k in range(1, cols):
        origin = lax.rem(z - k + cols, cols)
        arrive(big_ref.at[z], big_got.at[origin], big_send, big_recv, k, (r, origin))
        total = total + big_got[origin].astype(F32)
    big_out[r, z] = total.astype(BF16)
    for k in range(1, cols):
        go(big_out.at[r, z], big_out.at[r, z], bigc_send, bigc_recv, k, (r, lax.rem(z + k, cols)))

    total = small_ref[r].astype(F32)
    for k in range(1, rows):
        origin = lax.rem(r - k + rows, rows)
        arrive(small_ref.at[r], small_got.at[origin], small_send, small_recv, k, (origin, z))
        total = total + small_got[origin].astype(F32)
    small_col[z] = total.astype(BF16)
    for k in range(1, cols):
        go(small_col.at[z], small_col.at[z], smallc_send, smallc_recv, k, (r, lax.rem(z + k, cols)))

    for k in range(1, cols):
        origin = lax.rem(z - k + cols, cols)
        arrive(big_out.at[r, z], big_out.at[r, origin], bigc_send, bigc_recv, k, (r, origin))
    for k in range(1, rows):
        go(big_out.at[r], big_out.at[r], bigr_send, bigr_recv, k, (lax.rem(r + k, rows), z))

    for k in range(1, cols):
        origin = lax.rem(z - k + cols, cols)
        arrive(small_col.at[z], small_col.at[origin], smallc_send, smallc_recv, k, (r, origin))
    total = small_col[0].astype(F32)
    for at in range(1, cols):
        total = total + small_col[at].astype(F32)
    small_out[r] = total.astype(BF16)
    for k in range(1, rows):
        go(small_out.at[r], small_out.at[r], smallr_send, smallr_recv, k, (lax.rem(r + k, rows), z))

    for k in range(1, rows):
        origin = lax.rem(r - k + rows, rows)
        arrive(big_out.at[r], big_out.at[origin], bigr_send, bigr_recv, k, (origin, z))
        arrive(small_out.at[r], small_out.at[origin], smallr_send, smallr_recv, k, (origin, z))
    for copy in started:
        copy.wait_send()


def total_weights(rows, cols, big, small):
    by_row = [pltpu.SemaphoreType.DMA((rows,))] * 2
    by_col = [pltpu.SemaphoreType.DMA((cols,))] * 2
    return pl.pallas_call(
        functools.partial(total_kernel, rows, cols),
        out_shape=(
            jax.ShapeDtypeStruct((rows,) + big.shape, big.dtype),
            jax.ShapeDtypeStruct(small.shape, small.dtype),
        ),
        in_specs=[VM] * 2,
        out_specs=(VM,) * 2,
        scratch_shapes=[
            pltpu.VMEM(big.shape, big.dtype),
            pltpu.VMEM(small.shape, small.dtype),
            pltpu.VMEM((cols,) + small.shape[1:], small.dtype),
        ]
        + by_col + by_row + by_col + by_col + by_row + by_row,
        compiler_params=pltpu.CompilerParams(
            collective_id=2, has_side_effects=True, vmem_limit_bytes=24 << 20
        ),
    )(big, small)


def mm(a, b):
    return lax.dot_general(a, b, (((1,), (0,)), ((), ())), preferred_element_type=F32)


def mm_t(a, b):
    return lax.dot_general(a, b, (((1,), (1,)), ((), ())), preferred_element_type=F32)


def pair_kernel(
    scale, channels, span, fold, blocks,
    l_ref, lt_ref, b_ref, w_ref, wt_ref, off_ref, gain_ref, ex_ref, ext_ref, co_ref, cot_ref,
    pair_ref, up_ref,
    res_ref, grad_ref, dl_ref, dr_ref, gw_ref,
    o_s, d_s, gw_s, dl_s, dr_s,
):
    groups = o_s.shape[0]
    seqs = l_ref.shape[1] // fold
    cc = w_ref.shape[0]
    width = w_ref.shape[1]
    hid = co_ref.shape[0]
    lane = fold * span

    def outer_step(t, carry):
        e = t * 2
        part = mm_t(l_ref[...], b_ref[pl.ds(pl.multiple_of(e * lane, 2 * lane), 2 * lane), :])
        part = (part * scale).astype(BF16)
        for h in range(2):
            at = pl.multiple_of((e + h) * channels, channels)
            o_s[:, pl.ds(at, channels), :] = part[:, h * lane : (h + 1) * lane].reshape(
                groups, channels, lane
            )
        return carry

    lax.fori_loop(0, channels // 2, outer_step, 0)

    gw_s[...] = jnp.zeros_like(gw_s)
    many = blocks * lane

    def pair_step(q, carry):
        rows = pl.ds(pl.multiple_of(q * many, many), many)
        outer = jnp.concatenate([o_s[q * blocks + h] for h in range(blocks)], axis=1)
        up = up_ref[rows, :]
        up_t = up.astype(F32).T
        up_tb = up_t.astype(BF16)
        pair_t = pair_ref[rows, :].astype(F32).T
        mid = (pair_t + (mm(wt_ref[...], outer) + off_ref[...])).astype(BF16).astype(F32)
        centred = mid - jnp.mean(mid, axis=0, keepdims=True)
        inv = lax.rsqrt(jnp.mean(centred * centred, axis=0, keepdims=True) + EPSILON)
        hat = centred * inv
        normed = (hat * gain_ref[...]).astype(BF16)
        pre = mm(ext_ref[...], normed)
        half = 0.5 * (1.0 + lax.erf(pre * ROOT_HALF))
        hidden = (pre * half).astype(BF16)
        slope = half + pre * jnp.exp(-0.5 * pre * pre) * INV_ROOT_TWO_PI
        res = mid + mm(cot_ref[...], hidden)
        res_ref[rows, :] = res.T.astype(BF16)
        gw_s[pl.ds(cc, hid), :] += mm(hidden, up)
        d_hid = (mm(co_ref[...], up_tb) * slope).astype(BF16)
        gw_s[pl.ds(cc + hid, hid), :] += mm_t(d_hid, normed)
        scaled = mm(ex_ref[...], d_hid) * gain_ref[...]
        grad = up_t + inv * (
            scaled
            - jnp.mean(scaled, axis=0, keepdims=True)
            - hat * jnp.mean(scaled * hat, axis=0, keepdims=True)
        )
        grad_tb = grad.astype(BF16)
        grad_ref[rows, :] = grad.T.astype(BF16)
        gw_s[pl.ds(0, cc), :] += mm_t(outer, grad_tb)
        d_out = mm(w_ref[...], grad_tb).astype(BF16)
        for h in range(blocks):
            d_s[q * blocks + h] = d_out[:, h * lane : (h + 1) * lane]
        return carry

    lax.fori_loop(0, groups // blocks, pair_step, 0)

    dl_s[...] = jnp.zeros_like(dl_s)
    shard = dr_s.shape[1] // channels
    lanes_at = lax.broadcasted_iota(jnp.int32, (seqs, lane), 1)

    def back_step(t, carry):
        e = t * 2
        both = [
            d_s[:, pl.ds(pl.multiple_of((e + h) * channels, channels), channels), :].reshape(
                groups * channels, lane
            )
            for h in range(2)
        ]
        both = jnp.concatenate(both, axis=1)
        dl_s[...] += mm(both, b_ref[pl.ds(pl.multiple_of(e * lane, 2 * lane), 2 * lane), :])
        right = mm(lt_ref[...], both)
        for h in range(2):
            mine = right[:seqs, h * lane : (h + 1) * lane]
            for f in range(1, fold):
                mine = jnp.where(
                    lanes_at >= f * span,
                    right[f * seqs : (f + 1) * seqs, h * lane : (h + 1) * lane],
                    mine,
                )
            turned = mine.T * scale
            out = turned[:span]
            for f in range(1, fold):
                out = out + turned[f * span : (f + 1) * span]
            at = pl.multiple_of((e + h) * shard, shard)
            dr_s[:, pl.ds(at, shard), :] = out.reshape(span // shard, shard, seqs)
        return carry

    lax.fori_loop(0, channels // 2, back_step, 0)
    dl_ref[...] = (dl_s[...] * scale).astype(BF16)
    dr_ref[...] = dr_s[...].astype(BF16)
    gw_ref[...] = gw_s[...].astype(BF16)


def on_device(
    alignment_tensor,
    alignment_scaling_vector,
    first_factor_matrix,
    second_factor_matrix,
    final_mapping_matrix,
    final_offset_vector,
    couple_tensor,
    feedforward_scaling_vector,
    feedforward_expand_matrix,
    feedforward_contract_matrix,
    upstream_sensitivity,
):
    seqs, shard, features = alignment_tensor.shape
    channels = first_factor_matrix.shape[1]
    row_count, col_count, width = couple_tensor.shape
    hid = feedforward_contract_matrix.shape[0]
    rows = lax.axis_size("row")
    cols = lax.axis_size("col")
    amino_number = row_count * rows
    fold = max(1, LANES // col_count)
    lane = fold * col_count
    groups = row_count // fold
    local_groups = shard // fold
    pairs = row_count * col_count
    cc = channels * channels

    full, msa_hat, msa_inv = standardize_features(
        alignment_tensor.astype(F32), alignment_scaling_vector
    )
    normed = full.astype(BF16)
    left = jnp.einsum("srm,mc->rcs", normed, first_factor_matrix, preferred_element_type=F32)
    left = left.astype(BF16).reshape(local_groups, fold, channels, seqs)
    left = left.transpose(0, 2, 1, 3).reshape(local_groups * channels, fold * seqs)
    right = jnp.einsum("srm,me->ers", normed, second_factor_matrix, preferred_element_type=F32)
    right = right.astype(BF16).reshape(channels * shard, seqs)

    left_all, right_all = gather_sides(rows, cols, left, right)
    left_all = left_all.reshape(groups * channels, fold * seqs)
    side = right_all.reshape(rows, channels, shard, seqs).transpose(1, 0, 2, 3)
    side = side.reshape(channels, col_count, seqs)
    diagonal = jnp.concatenate(
        [
            jnp.pad(side, ((0, 0), (0, 0), (f * seqs, (fold - 1 - f) * seqs)))
            for f in range(fold)
        ],
        axis=1,
    ).reshape(channels * lane, fold * seqs)

    mapping = final_mapping_matrix.reshape(channels, channels, width)
    mapping = mapping.transpose(1, 0, 2).reshape(cc, width)
    blocks = 2 if groups % 2 == 0 else 1
    weight_rows = cc + 2 * hid
    results, grads, left_part, right_part, weight_part = pl.pallas_call(
        functools.partial(pair_kernel, 1.0 / seqs, channels, col_count, fold, blocks),
        out_shape=(
            jax.ShapeDtypeStruct((pairs, width), BF16),
            jax.ShapeDtypeStruct((pairs, width), BF16),
            jax.ShapeDtypeStruct((groups * channels, fold * seqs), BF16),
            jax.ShapeDtypeStruct((rows, channels * shard, seqs), BF16),
            jax.ShapeDtypeStruct((weight_rows, width), BF16),
        ),
        in_specs=[VM] * 13,
        out_specs=(VM,) * 5,
        scratch_shapes=[
            pltpu.VMEM((groups, cc, lane), BF16),
            pltpu.VMEM((groups, cc, lane), BF16),
            pltpu.VMEM((weight_rows, width), F32),
            pltpu.VMEM((groups * channels, fold * seqs), F32),
            pltpu.VMEM((rows, channels * shard, seqs), F32),
        ],
        compiler_params=pltpu.CompilerParams(vmem_limit_bytes=60 << 20),
    )(
        left_all,
        left_all.T,
        diagonal,
        mapping,
        mapping.T,
        final_offset_vector.reshape(width, 1),
        feedforward_scaling_vector.reshape(width, 1),
        feedforward_expand_matrix,
        feedforward_expand_matrix.T,
        feedforward_contract_matrix,
        feedforward_contract_matrix.T,
        couple_tensor.reshape(pairs, width),
        upstream_sensitivity.reshape(pairs, width),
    )

    left_got, right_grad, big = scatter_grads(
        rows,
        cols,
        left_part.reshape(cols, local_groups * channels, fold * seqs),
        right_part,
        weight_part.reshape(rows, weight_rows // rows, width),
    )
    left_grad = jnp.sum(left_got.astype(F32), axis=0).astype(BF16)
    left_grad = left_grad.reshape(local_groups, channels, fold, seqs)
    left_grad = left_grad.transpose(0, 2, 1, 3).reshape(shard, channels, seqs)
    right_grad = right_grad.reshape(channels, shard, seqs).transpose(1, 0, 2)
    both_grad = jnp.concatenate([left_grad, right_grad], axis=1)
    both_factor = jnp.concatenate([first_factor_matrix, second_factor_matrix], axis=1)
    both_weight = jnp.einsum("srm,rcs->cm", normed, both_grad, preferred_element_type=F32)
    incoming = jnp.einsum("rcs,mc->srm", both_grad, both_factor, preferred_element_type=F32)
    alignment_sensitivity = standardize_reverse_mode(
        incoming, msa_hat, msa_inv, alignment_scaling_vector
    ).astype(BF16)

    small_rows = 2 * channels * features // width
    each = -(-small_rows // (rows * 16)) * 16
    small = both_weight.astype(BF16).reshape(small_rows, width)
    small = jnp.pad(small, ((0, each * rows - small_rows), (0, 0)))
    big_all, small_all = total_weights(
        rows,
        cols,
        big.reshape(cols, weight_rows // (rows * cols), width),
        small.reshape(rows, each, width),
    )
    big_all = big_all.reshape(weight_rows, width)
    small_all = small_all.reshape(each * rows, width)[:small_rows]
    small_all = small_all.reshape(2, channels, features).astype(F32) / amino_number
    out_proj = big_all[:cc].reshape(channels, channels, width).transpose(1, 0, 2)
    return (
        results.reshape(row_count, col_count, width),
        grads.reshape(row_count, col_count, width),
        alignment_sensitivity,
        out_proj.reshape(cc, width).astype(F32) / amino_number,
        big_all[cc + hid :].T.astype(F32) / amino_number,
        big_all[cc : cc + hid].astype(F32) / amino_number,
        small_all[0].T,
        small_all[1].T,
    )


def solution(mesh):
    pair_spec = P("row", "col", None)
    msa_spec = P(None, ("row", "col"), None)
    return jax.shard_map(
        on_device,
        mesh=mesh,
        in_specs=(
            msa_spec, P(), P(), P(), P(), P(), pair_spec, P(), P(), P(), pair_spec,
        ),
        out_specs=(pair_spec, pair_spec, msa_spec, P(), P(), P(), P(), P()),
        check_vma=False,
    )
```

time: 596 us -> 102 us (0.17)
  waiting for transfers between devices: 411 us -> 0 us
  Pallas kernels: 0 us -> 78.4 us
  matrix products: 63.4 us -> 1.33 us
  local copies, waits for them, and re-layouts: 78.1 us -> 18.1 us
  between operations: 14.4 us -> 0.89 us
  loops' own time: 9.79 us -> 0 us
  other arithmetic: 12.2 us -> 3.01 us
    psum x2 -> x0, waiting for transfers between devices: 247 us -> none  [on_device(): lax.psum((summed_result_state, summed_entry_state, summed_feedforward_res...]
    all_gather x2 -> x0, waiting for transfers between devices: 116 us -> none  [the longest x1 58 us: on_device(): lax.all_gather(right_local, ('row', 'col'), axis=0, tiled=True)]
    pallas_call x0 -> x4, Pallas kernels: none -> 78.4 us  [the longest x1 26.1 us: on_device(): pl.pallas_call(functools.partial(pair_kernel, 1.0 / seqs, channels, col_c...]
    dot_general x54 -> x4, matrix products: 63.4 us -> 1.33 us  [the longest x1 0.39 us: on_device(): jnp.einsum('rcs,mc->srm', both_grad, both_factor, preferred_element_type=...]
    reduce_scatter x2 -> x0, waiting for transfers between devices: 47.6 us -> none  [the longest x1 32.7 us: on_device(): lax.psum_scatter(routed.astype(jnp.bfloat16), 'row', scatter_dimension=0,...]
    reshape x16 -> x9, local copies, waits for them, and re-layouts: 41.9 us -> 4.71 us  [the longest x1 1.39 us: on_device(): final_offset_vector.reshape(width, 1)]
    dynamic_slice x14 -> x0, local copies, waits for them, and re-layouts: 12.4 us -> none  [the longest x4 3.68 us: block_step(): lax.dynamic_slice_in_dim(upstream_sensitivity, start_row, block_rows, 0)]
    another operation x1 -> x0, loops' own time: 9.79 us -> none  [on_device(): totals, stacked = lax.scan(block_step, initial, starts)]
  transfers between devices with their start and end apart: 7 -> 0, of which waited for: 6 -> 0; matrix products, arithmetic and copies ran while one was open for 3% -> 0% of each run, Pallas kernels for 0% -> 0%
where the time goes in v1:
time: 102 us
  Pallas kernels  78.4 us (77%)
  local copies, waits for them, and re-layouts  18.1 us (18%)
  other arithmetic  3.01 us (3%)
  matrix products  1.33 us (1%)
    pallas_call x1, Pallas kernels, on_device(): pl.pallas_call(functools.partial(pair_kernel, 1.0 / seqs, channels, col_c...  26.1 us
    pallas_call x1, Pallas kernels, gather_sides(): pl.pallas_call(functools.partial(gather_kernel, rows, cols), out_shape=(j...  19.1 us
    pallas_call x1, Pallas kernels, total_weights(): pl.pallas_call(functools.partial(total_kernel, rows, cols), out_shape=(ja...  18.5 us
    pallas_call x1, Pallas kernels, scatter_grads(): pl.pallas_call(functools.partial(scatter_kernel, rows, cols), out_shape=(...  14.7 us
    unnamed x21, local copies, waits for them, and re-layouts  9.05 us

profile of v1, /device:TPU:0, one launch (start us, length us, event | category | flops | bytes accessed | tf_op | source)
XLA Modules:
  0.0 101.7 jit_solution(6251030851010018431)
XLA Ops:
  0.6 0.0 copy-start.7
  0.6 0.0 copy-start.5
  0.7 1.4 %copy.69.off_ref = f32[128,1]{1,0:T(8,128)} copy(f32[128,1]{0,1:T(1,128)} %bitcast.104) | data formatting | bytes 1024 | tf_op jit(solution)/shard_map/reshape | solution.py:569
  2.0 1.4 %copy.70.gain_ref = f32[128,1]{1,0:T(8,128)} copy(f32[128,1]{0,1:T(1,128)} %bitcast.105) | data formatting | bytes 1024 | tf_op jit(solution)/shard_map/reshape | solution.py:570
  3.4 1.7 %copy.66 = bf16[128,512]{0,1:T(8,128)(2,1)} copy(bf16[128,512]{1,0:T(8,128)(2,1)} %ex_ref.1) | data formatting | bytes 262144 | tf_op args[8]
  5.1 1.7 %copy.67 = bf16[512,128]{0,1:T(8,128)(2,1)} copy(bf16[512,128]{1,0:T(8,128)(2,1)} %co_ref.1) | data formatting | bytes 262144 | tf_op args[9]
  6.7 1.1 %copy.64 = bf16[32,32,128]{2,1,0:T(8,128)(2,1)S(1)} copy(bf16[32,32,128]{2,0,1:T(8,128)(2,1)} %bitcast.93) | data formatting | bytes 524288 | tf_op jit(solution)/shard_map/transpose | solution.py:541
  7.8 0.0 copy-start.4
  7.8 0.0 copy-start.6
  7.8 0.9 copy.65
  8.7 1.5 %copy.57 = bf16[128,8,256]{0,2,1:T(8,128)(2,1)S(1)} copy(bf16[128,8,256]{2,1,0:T(8,128)(2,1)} %param.11) | data formatting | bytes 1048576 | tf_op args[0]
  10.1 0.1 convert_reduce_fusion
  10.2 0.1 fusion.16
  10.4 0.0 copy-done.7
  10.4 0.0 copy-done.5
  10.4 0.3 convolution_convert_fusion.1
  10.7 0.1 copy.59
  10.8 0.0 copy-done.6
  10.8 0.3 fusion.9
  11.1 0.0 copy-done.4
  11.2 19.1 %shard_map.170 = (bf16[4,128,256]{2,1,0:T(8,128)(2,1)S(1)}, bf16[8,256,128]{2,1,0:T(8,128)(2,1)S(1)}) custom-call(bf16[128,256]{1,0:T(8,128)(2,1)S(1)} %bitcast.76, bf16[256,128]{1,0:T(8,128)(2,1)S(1)} %bitcast.77), custom_call_target="tpu_custom_call" | custom-call | tf_op jit(solution)/shard_map/pallas_call | solution.py:147
  30.3 0.0 copy-start
  30.3 0.8 copy.80
  31.1 0.1 copy_bitcast_fusion
  31.3 1.6 %fusion.2 = bf16[32,128,256]{2,1,0:T(8,128)(2,1)} fusion(bf16[32,64,128]{2,1,0:T(8,128)(2,1)S(1)} %copy_bitcast_fusion), kind=kLoop, calls=%fused_computation.4 | loop fusion | flops 8388608 | bytes 2621440 | tf_op jit(solution)/shard_map/concatenate | solution.py:532
  32.9 0.0 copy-done
  32.9 26.1 %shard_map.171 = (bf16[2048,128]{1,0:T(8,128)(2,1)}, bf16[2048,128]{1,0:T(8,128)(2,1)}, bf16[512,256]{1,0:T(8,128)(2,1)}, bf16[8,256,128]{2,1,0:T(8,128)(2,1)}, bf16[2048,128]{1,0:T(8,128)(2,1)}) custom-call(bf16[512,256]{1,0:T(8,128)(2,1)} %bitcast.73, bf16[256,512]{1,0:T(8,128)(2,1)} %bitcast.85, bf16[4096,256]{1,0:T(8,128)(2,1)} %bitcast.80, ...), custom_call_target="tpu_custom_call" | custom-call | tf_op jit(solution)/shard_map/pallas_call | solution.py:544
  59.0 0.0 copy-start.1
  59.0 1.0 %copy-done.1 = bf16[8,256,128]{2,1,0:T(8,128)(2,1)S(1)} copy-done((bf16[8,256,128]{2,1,0:T(8,128)(2,1)S(1)}, bf16[8,256,128]{2,1,0:T(8,128)(2,1)}, u32[]{:S(2)}) %copy-start.1) | copy-done | bytes 524312
  60.1 0.0 copy-start.2
  60.1 1.0 %copy-done.2 = bf16[2048,128]{1,0:T(8,128)(2,1)S(1)} copy-done((bf16[2048,128]{1,0:T(8,128)(2,1)S(1)}, bf16[2048,128]{1,0:T(8,128)(2,1)}, u32[]{:S(2)}) %copy-start.2) | copy-done | bytes 524312
  61.1 0.0 copy-start.3
  61.1 0.9 copy-done.3
  62.1 14.7 %shard_map.172 = (bf16[4,128,256]{2,1,0:T(8,128)(2,1)S(1)}, bf16[256,128]{1,0:T(8,128)(2,1)S(1)}, bf16[256,128]{1,0:T(8,128)(2,1)S(1)}) custom-call(bf16[4,128,256]{2,1,0:T(8,128)(2,1)S(1)} %bitcast.75, bf16[8,256,128]{2,1,0:T(8,128)(2,1)S(1)} %copy-done.1, bf16[8,256,128]{2,1,0:T(8,128)(2,1)S(1)} %bitcast.74), custom_call_target="tpu_custom_call" | custom-call | tf_op jit(solution)/shard_map/pallas_call | solution.py:259
  76.9 0.3 fusion.10
  77.3 18.5 %shard_map.173 = (bf16[8,4,64,128]{3,2,1,0:T(8,128)(2,1)S(1)}, bf16[8,16,128]{2,1,0:T(8,128)(2,1)S(1)}) custom-call(bf16[4,64,128]{2,1,0:T(8,128)(2,1)S(1)} %bitcast.78, bf16[8,16,128]{2,1,0:T(8,128)(2,1)S(1)} %reshape.152.small_ref), custom_call_target="tpu_custom_call" | custom-call | tf_op jit(solution)/shard_map/pallas_call | solution.py:359
  95.8 0.6 squeeze.7
  96.4 0.6 squeeze.6
  97.1 1.1 %copy.74 = f32[32,32,128]{2,1,0:T(8,128)} copy(f32[32,32,128]{2,0,1:T(8,128)S(1)} %bitcast.83) | data formatting | bytes 1048576 | tf_op jit(solution)/shard_map/div | solution.py:616
  98.2 0.8 convert_multiply_fusion.1
  99.0 0.8 copy.75
  99.8 0.4 fusion.26
  100.2 0.3 fusion.15
  100.5 1.2 %copy.76 = bf16[128,8,256]{2,1,0:T(8,128)(2,1)} copy(bf16[128,8,256]{0,2,1:T(8,128)(2,1)S(1)} %fusion.15) | data formatting | bytes 1048576
  (13 shorter events, 0.2 us)
Async XLA Ops:
  0.6 9.8 %copy-start.7 = (f32[256]{0:T(256)S(1)}, f32[256]{0:T(256)}, u32[]{:S(2)}) copy-start(f32[256]{0:T(256)} %param.12) | copy-start | bytes 3076
  0.6 9.8 %copy-start.5 = (bf16[256,32]{0,1:T(8,128)(2,1)S(1)}, bf16[256,32]{0,1:T(8,128)(2,1)}, u32[]{:S(2)}) copy-start(bf16[256,32]{0,1:T(8,128)(2,1)} %param.13) | copy-start | bytes 49156
  7.8 3.3 %copy-start.4 = (bf16[32,32,128]{2,1,0:T(8,128)(2,1)}, bf16[32,32,128]{2,1,0:T(8,128)(2,1)S(1)}, u32[]{:S(2)}) copy-start(bf16[32,32,128]{2,1,0:T(8,128)(2,1)S(1)} %copy.64) | copy-start | bytes 786436
  7.8 3.0 %copy-start.6 = (bf16[256,32]{0,1:T(8,128)(2,1)S(1)}, bf16[256,32]{0,1:T(8,128)(2,1)}, u32[]{:S(2)}) copy-start(bf16[256,32]{0,1:T(8,128)(2,1)} %param.14) | copy-start | bytes 49156
  30.3 2.6 %copy-start = (bf16[4,128,256]{2,1,0:T(8,128)(2,1)}, bf16[4,128,256]{2,1,0:T(8,128)(2,1)S(1)}, u32[]{:S(2)}) copy-start(bf16[4,128,256]{2,1,0:T(8,128)(2,1)S(1)} %get-tuple-element.20) | copy-start | bytes 786436
  59.0 1.0 %copy-start.1 = (bf16[8,256,128]{2,1,0:T(8,128)(2,1)S(1)}, bf16[8,256,128]{2,1,0:T(8,128)(2,1)}, u32[]{:S(2)}) copy-start(bf16[8,256,128]{2,1,0:T(8,128)(2,1)} %get-tuple-element.25.right_ref) | copy-start | bytes 1572868
  60.1 1.0 %copy-start.2 = (bf16[2048,128]{1,0:T(8,128)(2,1)S(1)}, bf16[2048,128]{1,0:T(8,128)(2,1)}, u32[]{:S(2)}) copy-start(bf16[2048,128]{1,0:T(8,128)(2,1)} %get-tuple-element.26) | copy-start | bytes 1572868
  61.1 0.9 copy-start.3

commit v2 on v1

--- a/solution.py
+++ b/solution.py
@@ -1,4 +1,5 @@
 import functools
+import math
 
 import jax
 import jax.numpy as jnp
@@ -386,10 +387,9 @@
 
 def pair_kernel(
     scale, channels, span, fold, blocks,
-    l_ref, lt_ref, b_ref, w_ref, wt_ref, off_ref, gain_ref, ex_ref, ext_ref, co_ref, cot_ref,
-    pair_ref, up_ref,
+    l_ref, r_ref, map_ref, off_ref, gain_ref, ex_ref, co_ref, pair_ref, up_ref,
     res_ref, grad_ref, dl_ref, dr_ref, gw_ref,
-    o_s, d_s, gw_s, dl_s, dr_s,
+    o_s, d_s, gw_s, dl_s, dr_s, b_ref, lt_ref, w_ref, wt_ref, ext_ref, cot_ref, vec_s,
 ):
     groups = o_s.shape[0]
     seqs = l_ref.shape[1] // fold
@@ -397,9 +397,33 @@
     width = w_ref.shape[1]
     hid = co_ref.shape[0]
     lane = fold * span
+    shard = dr_s.shape[1] // channels
+
+    gw_s[pl.ds(0, cc), :] = map_ref[...].astype(F32)
+    for e in range(channels):
+        w_ref[pl.ds(e * channels, channels), :] = gw_s[
+            pl.ds(e, channels, stride=channels), :
+        ].astype(BF16)
+    wt_ref[...] = w_ref[...].astype(F32).T.astype(BF16)
+    ext_ref[...] = ex_ref[...].astype(F32).T.astype(BF16)
+    cot_ref[...] = co_ref[...].astype(F32).T.astype(BF16)
+    lt_ref[...] = l_ref[...].astype(F32).T.astype(BF16)
+    vec_s[0] = jnp.broadcast_to(off_ref[...], (width, width)).T
+    vec_s[1] = jnp.broadcast_to(gain_ref[...], (width, width)).T
+    off = vec_s[0][:, :1]
+    gain = vec_s[1][:, :1]
+    dr_s[...] = r_ref[...].astype(F32)
+    none = jnp.zeros((span, seqs), BF16)
 
     def outer_step(t, carry):
         e = t * 2
+        for h in range(2):
+            at = pl.multiple_of((e + h) * shard, shard)
+            side = dr_s[:, pl.ds(at, shard), :].reshape(span, seqs).astype(BF16)
+            for f in range(fold):
+                b_ref[
+                    pl.ds(pl.multiple_of((e + h) * lane + f * span, span), span), :
+                ] = jnp.concatenate([side if k == f else none for k in range(fold)], axis=1)
         part = mm_t(l_ref[...], b_ref[pl.ds(pl.multiple_of(e * lane, 2 * lane), 2 * lane), :])
         part = (part * scale).astype(BF16)
         for h in range(2):
@@ -421,11 +445,11 @@
         up_t = up.astype(F32).T
         up_tb = up_t.astype(BF16)
         pair_t = pair_ref[rows, :].astype(F32).T
-        mid = (pair_t + (mm(wt_ref[...], outer) + off_ref[...])).astype(BF16).astype(F32)
+        mid = (pair_t + (mm(wt_ref[...], outer) + off)).astype(BF16).astype(F32)
         centred = mid - jnp.mean(mid, axis=0, keepdims=True)
         inv = lax.rsqrt(jnp.mean(centred * centred, axis=0, keepdims=True) + EPSILON)
         hat = centred * inv
-        normed = (hat * gain_ref[...]).astype(BF16)
+        normed = (hat * gain).astype(BF16)
         pre = mm(ext_ref[...], normed)
         half = 0.5 * (1.0 + lax.erf(pre * ROOT_HALF))
         hidden = (pre * half).astype(BF16)
@@ -435,7 +459,7 @@
         gw_s[pl.ds(cc, hid), :] += mm(hidden, up)
         d_hid = (mm(co_ref[...], up_tb) * slope).astype(BF16)
         gw_s[pl.ds(cc + hid, hid), :] += mm_t(d_hid, normed)
-        scaled = mm(ex_ref[...], d_hid) * gain_ref[...]
+        scaled = mm(ex_ref[...], d_hid) * gain
         grad = up_t + inv * (
             scaled
             - jnp.mean(scaled, axis=0, keepdims=True)
@@ -452,7 +476,6 @@
     lax.fori_loop(0, groups // blocks, pair_step, 0)
 
     dl_s[...] = jnp.zeros_like(dl_s)
-    shard = dr_s.shape[1] // channels
     lanes_at = lax.broadcasted_iota(jnp.int32, (seqs, lane), 1)
 
     def back_step(t, carry):
@@ -485,7 +508,22 @@
     lax.fori_loop(0, channels // 2, back_step, 0)
     dl_ref[...] = (dl_s[...] * scale).astype(BF16)
     dr_ref[...] = dr_s[...].astype(BF16)
-    gw_ref[...] = gw_s[...].astype(BF16)
+    for c in range(channels):
+        gw_ref[pl.ds(c * channels, channels), :] = gw_s[
+            pl.ds(c, channels, stride=channels), :
+        ].astype(BF16)
+    gw_ref[pl.ds(cc, 2 * hid), :] = gw_s[pl.ds(cc, 2 * hid), :].astype(BF16)
+
+
+def finish_kernel(scale, channels, cc, hid, big_ref, small_ref, o_ref, in_ref, out_ref, f_ref, s_ref):
+    o_ref[...] = big_ref[pl.ds(0, cc), :].astype(F32) * scale
+    out_ref[...] = big_ref[pl.ds(cc, hid), :].astype(F32) * scale
+    in_ref[...] = big_ref[pl.ds(cc + hid, hid), :].astype(F32).T * scale
+    width = small_ref.shape[1]
+    for h in range(f_ref.shape[0] // width):
+        part = small_ref[pl.ds(h * 2 * channels, 2 * channels), :].astype(F32).T * scale
+        f_ref[pl.ds(h * width, width), :] = part[:, :channels]
+        s_ref[pl.ds(h * width, width), :] = part[:, channels:]
 
 
 def on_device(
@@ -526,52 +564,46 @@
     right = right.astype(BF16).reshape(channels * shard, seqs)
 
     left_all, right_all = gather_sides(rows, cols, left, right)
-    left_all = left_all.reshape(groups * channels, fold * seqs)
-    side = right_all.reshape(rows, channels, shard, seqs).transpose(1, 0, 2, 3)
-    side = side.reshape(channels, col_count, seqs)
-    diagonal = jnp.concatenate(
-        [
-            jnp.pad(side, ((0, 0), (0, 0), (f * seqs, (fold - 1 - f) * seqs)))
-            for f in range(fold)
-        ],
-        axis=1,
-    ).reshape(channels * lane, fold * seqs)
-
-    mapping = final_mapping_matrix.reshape(channels, channels, width)
-    mapping = mapping.transpose(1, 0, 2).reshape(cc, width)
     blocks = 2 if groups % 2 == 0 else 1
     weight_rows = cc + 2 * hid
+    outs = (
+        jax.ShapeDtypeStruct((pairs, width), BF16),
+        jax.ShapeDtypeStruct((pairs, width), BF16),
+        jax.ShapeDtypeStruct((groups * channels, fold * seqs), BF16),
+        jax.ShapeDtypeStruct((rows, channels * shard, seqs), BF16),
+        jax.ShapeDtypeStruct((weight_rows, width), BF16),
+    )
+    scratch = [
+        ((groups, cc, lane), BF16),
+        ((groups, cc, lane), BF16),
+        ((weight_rows, width), F32),
+        ((groups * channels, fold * seqs), F32),
+        ((rows, channels * shard, seqs), F32),
+        ((channels * lane, fold * seqs), BF16),
+        ((fold * seqs, groups * channels), BF16),
+        ((cc, width), BF16),
+        ((width, cc), BF16),
+        ((hid, width), BF16),
+        ((width, hid), BF16),
+        ((2, width, width), F32),
+    ]
+    space = sum(math.prod(shape) * jnp.dtype(kind).itemsize for shape, kind in scratch)
+    space += 2 * sum(math.prod(out.shape) * 2 for out in outs)
     results, grads, left_part, right_part, weight_part = pl.pallas_call(
         functools.partial(pair_kernel, 1.0 / seqs, channels, col_count, fold, blocks),
-        out_shape=(
-            jax.ShapeDtypeStruct((pairs, width), BF16),
-            jax.ShapeDtypeStruct((pairs, width), BF16),
-            jax.ShapeDtypeStruct((groups * channels, fold * seqs), BF16),
-            jax.ShapeDtypeStruct((rows, channels * shard, seqs), BF16),
-            jax.ShapeDtypeStruct((weight_rows, width), BF16),
-        ),
-        in_specs=[VM] * 13,
+        out_shape=outs,
+        in_specs=[VM] * 9,
         out_specs=(VM,) * 5,
-        scratch_shapes=[
-            pltpu.VMEM((groups, cc, lane), BF16),
-            pltpu.VMEM((groups, cc, lane), BF16),
-            pltpu.VMEM((weight_rows, width), F32),
-            pltpu.VMEM((groups * channels, fold * seqs), F32),
-            pltpu.VMEM((rows, channels * shard, seqs), F32),
-        ],
-        compiler_params=pltpu.CompilerParams(vmem_limit_bytes=60 << 20),
+        scratch_shapes=[pltpu.VMEM(shape, kind) for shape, kind in scratch],
+        compiler_params=pltpu.CompilerParams(vmem_limit_bytes=min(60 << 20, space + (8 << 20))),
     )(
-        left_all,
-        left_all.T,
-        diagonal,
-        mapping,
-        mapping.T,
-        final_offset_vector.reshape(width, 1),
-        feedforward_scaling_vector.reshape(width, 1),
+        left_all.reshape(groups * channels, fold * seqs),
+        right_all,
+        final_mapping_matrix,
+        final_offset_vector.reshape(1, width),
+        feedforward_scaling_vector.reshape(1, width),
         feedforward_expand_matrix,
-        feedforward_expand_matrix.T,
         feedforward_contract_matrix,
-        feedforward_contract_matrix.T,
         couple_tensor.reshape(pairs, width),
         upstream_sensitivity.reshape(pairs, width),
     )
@@ -597,7 +629,8 @@
 
     small_rows = 2 * channels * features // width
     each = -(-small_rows // (rows * 16)) * 16
-    small = both_weight.astype(BF16).reshape(small_rows, width)
+    small = both_weight.astype(BF16).reshape(2 * channels, features // width, width)
+    small = small.transpose(1, 0, 2).reshape(small_rows, width)
     small = jnp.pad(small, ((0, each * rows - small_rows), (0, 0)))
     big_all, small_all = total_weights(
         rows,
@@ -605,19 +638,28 @@
         big.reshape(cols, weight_rows // (rows * cols), width),
         small.reshape(rows, each, width),
     )
-    big_all = big_all.reshape(weight_rows, width)
-    small_all = small_all.reshape(each * rows, width)[:small_rows]
-    small_all = small_all.reshape(2, channels, features).astype(F32) / amino_number
-    out_proj = big_all[:cc].reshape(channels, channels, width).transpose(1, 0, 2)
+    out_proj, trans_in, trans_out, first, second = pl.pallas_call(
+        functools.partial(finish_kernel, 1.0 / amino_number, channels, cc, hid),
+        out_shape=(
+            jax.ShapeDtypeStruct((cc, width), F32),
+            jax.ShapeDtypeStruct((width, hid), F32),
+            jax.ShapeDtypeStruct((hid, width), F32),
+            jax.ShapeDtypeStruct((features, channels), F32),
+            jax.ShapeDtypeStruct((features, channels), F32),
+        ),
+        in_specs=[VM] * 2,
+        out_specs=(VM,) * 5,
+        compiler_params=pltpu.CompilerParams(vmem_limit_bytes=16 << 20),
+    )(big_all.reshape(weight_rows, width), small_all.reshape(each * rows, width))
     return (
         results.reshape(row_count, col_count, width),
         grads.reshape(row_count, col_count, width),
         alignment_sensitivity,
-        out_proj.reshape(cc, width).astype(F32) / amino_number,
-        big_all[cc + hid :].T.astype(F32) / amino_number,
-        big_all[cc : cc + hid].astype(F32) / amino_number,
-        small_all[0].T,
-        small_all[1].T,
+        out_proj,
+        trans_in,
+        trans_out,
+        first,
+        second,
     )
 
 

time: 102 us -> 87.9 us (0.86)
  local copies, waits for them, and re-layouts: 18.1 us -> 6.1 us
  other arithmetic: 3.01 us -> 0.57 us
    reshape x6 -> x1, local copies, waits for them, and re-layouts: 4.62 us -> 0.01 us  [on_device(): both_weight.astype(BF16).reshape(2 * channels, features // width, width)]
    unnamed x21 -> x25, local copies, waits for them, and re-layouts: 9.05 us -> 5.97 us
    div x2 -> x0, local copies, waits for them, and re-layouts: 1.94 us -> none  [the longest x1 1.1 us: on_device(): out_proj.reshape(cc, width).astype(F32) / amino_number]
    concatenate x1 -> x0, other arithmetic: 1.63 us -> none  [on_device(): jnp.concatenate([jnp.pad(side, ((0, 0), (0, 0), (f * seqs, (fold - 1 - f)...]
    pallas_call x1, Pallas kernels: 26.1 us -> 24.7 us  [on_device(): pl.pallas_call(functools.partial(pair_kernel, 1.0 / seqs, channels, col_c...]
    squeeze x2 -> x0, local copies, waits for them, and re-layouts: 1.25 us -> none  [the longest x1 0.62 us: on_device(): small_all[1]]
    pallas_call x0 -> x1, Pallas kernels: none -> 1.07 us  [on_device(): pl.pallas_call(functools.partial(finish_kernel, 1.0 / amino_number, chann...]
    transpose x1 -> x0, local copies, waits for them, and re-layouts: 1.05 us -> none  [on_device(): mapping = mapping.transpose(1, 0, 2).reshape(cc, width)]
where the time goes in v2:
time: 87.9 us; the launch traced here: 87.6 us
  Pallas kernels  78.7 us (90%)
  local copies, waits for them, and re-layouts  6.1 us (7%)
  matrix products  1.33 us (2%)
    pallas_call x1, Pallas kernels, on_device(): pl.pallas_call(functools.partial(pair_kernel, 1.0 / seqs, channels, col_c...  24.7 us
    pallas_call x1, Pallas kernels, gather_sides(): pl.pallas_call(functools.partial(gather_kernel, rows, cols), out_shape=(j...  19.1 us
    pallas_call x1, Pallas kernels, total_weights(): pl.pallas_call(functools.partial(total_kernel, rows, cols), out_shape=(ja...  19 us
    pallas_call x1, Pallas kernels, scatter_grads(): pl.pallas_call(functools.partial(scatter_kernel, rows, cols), out_shape=(...  14.8 us
    unnamed x25, local copies, waits for them, and re-layouts  5.97 us

profile of v2, /device:TPU:0, one launch (start us, length us, event | category | flops | bytes accessed | tf_op | source)
XLA Modules:
  0.0 87.6 jit_solution(18111028295549165892)
XLA Ops:
  0.6 1.5 %copy.30 = bf16[128,8,256]{0,2,1:T(8,128)(2,1)S(1)} copy(bf16[128,8,256]{2,1,0:T(8,128)(2,1)} %param.11) | data formatting | bytes 1048576 | tf_op args[0]
  2.1 0.1 convert_reduce_fusion
  2.2 0.0 copy-start.7
  2.2 0.1 fusion.14
  2.4 0.0 copy-start.9
  2.4 0.5 copy-done.7
  2.9 0.1 copy-done.9
  3.1 0.3 convolution_convert_fusion.1
  3.3 0.0 copy-start.8
  3.4 0.0 copy-start.4
  3.4 0.1 copy.32
  3.4 0.0 copy-start.3
  3.5 0.6 copy-done.8
  4.1 0.0 copy-start
  4.1 0.0 copy-start.1
  4.1 0.3 fusion.6
  4.4 0.0 copy-start.2
  4.4 19.1 %shard_map.170 = (bf16[4,128,256]{2,1,0:T(8,128)(2,1)S(1)}, bf16[8,256,128]{2,1,0:T(8,128)(2,1)S(1)}) custom-call(bf16[128,256]{1,0:T(8,128)(2,1)S(1)} %bitcast.65, bf16[256,128]{1,0:T(8,128)(2,1)S(1)} %bitcast.66), custom_call_target="tpu_custom_call" | custom-call | tf_op jit(solution)/shard_map/pallas_call | solution.py:148
  23.5 0.0 copy-start.5
  23.6 0.0 copy-start.6
  23.6 0.0 copy-done.4
  23.6 0.0 copy-done.3
  23.6 0.0 copy-done
  23.6 0.0 copy-done.1
  23.6 0.0 copy-done.2
  23.6 0.6 copy-done.5
  24.2 0.0 copy-done.6
  24.2 24.7 %shard_map.171 = (bf16[2048,128]{1,0:T(8,128)(2,1)}, bf16[2048,128]{1,0:T(8,128)(2,1)}, bf16[512,256]{1,0:T(8,128)(2,1)S(1)}, bf16[8,256,128]{2,1,0:T(8,128)(2,1)S(1)}, bf16[2048,128]{1,0:T(8,128)(2,1)S(1)}) custom-call(bf16[512,256]{1,0:T(8,128)(2,1)S(1)} %bitcast.64, bf16[8,256,128]{2,1,0:T(8,128)(2,1)S(1)} %get-tuple-element.26.r_ref, ...), custom_call_target="tpu_custom_call" | custom-call | tf_op jit(solution)/shard_map/pallas_call | solution.py:592
  48.9 14.8 %shard_map.172 = (bf16[4,128,256]{2,1,0:T(8,128)(2,1)S(1)}, bf16[256,128]{1,0:T(8,128)(2,1)S(1)}, bf16[256,128]{1,0:T(8,128)(2,1)S(1)}) custom-call(bf16[4,128,256]{2,1,0:T(8,128)(2,1)S(1)} %bitcast.63, bf16[8,256,128]{2,1,0:T(8,128)(2,1)S(1)} %get-tuple-element.30.right_ref, bf16[8,256,128]{2,1,0:T(8,128)(2,1)S(1)} %bitcast.59), custom_call_target="tpu_custom_call" | custom-call | tf_op jit(solution)/shard_map/pallas_call | solution.py:260
  63.9 0.4 fusion.24
  64.3 0.3 fusion.13
  64.6 1.2 %copy.39 = bf16[128,8,256]{2,1,0:T(8,128)(2,1)} copy(bf16[128,8,256]{0,2,1:T(8,128)(2,1)S(1)} %fusion.13) | data formatting | bytes 1048576
  65.8 0.4 fusion.8
  66.1 19.0 %shard_map.173 = (bf16[8,4,64,128]{3,2,1,0:T(8,128)(2,1)S(1)}, bf16[8,16,128]{2,1,0:T(8,128)(2,1)S(1)}) custom-call(bf16[4,64,128]{2,1,0:T(8,128)(2,1)S(1)} %bitcast.68, bf16[8,16,128]{2,1,0:T(8,128)(2,1)S(1)} %bitcast.67), custom_call_target="tpu_custom_call" | custom-call | tf_op jit(solution)/shard_map/pallas_call | solution.py:360
  85.1 1.1 %shard_map.174 = (f32[1024,128]{1,0:T(8,128)}, f32[128,512]{1,0:T(8,128)}, f32[512,128]{1,0:T(8,128)}, f32[256,32]{1,0:T(8,128)S(1)}, f32[256,32]{1,0:T(8,128)S(1)}) custom-call(bf16[2048,128]{1,0:T(8,128)(2,1)S(1)} %bitcast.60, bf16[128,128]{1,0:T(8,128)(2,1)S(1)} %bitcast.70), custom_call_target="tpu_custom_call" | custom-call | tf_op jit(solution)/shard_map/pallas_call | solution.py:641
  86.2 0.7 copy.40
  86.9 0.7 copy.41
  (10 shorter events, 0.1 us)
Async XLA Ops:
  2.2 0.7 copy-start.7
  2.4 0.7 copy-start.9
  3.3 0.7 copy-start.8
  3.4 20.2 %copy-start.4 = (bf16[512,128]{1,0:T(8,128)(2,1)S(1)}, bf16[512,128]{1,0:T(8,128)(2,1)}, u32[]{:S(2)}) copy-start(bf16[512,128]{1,0:T(8,128)(2,1)} %co_ref.1) | copy-start | bytes 393220
  3.4 20.2 %copy-start.3 = (bf16[128,512]{1,0:T(8,128)(2,1)S(1)}, bf16[128,512]{1,0:T(8,128)(2,1)}, u32[]{:S(2)}) copy-start(bf16[128,512]{1,0:T(8,128)(2,1)} %ex_ref.1) | copy-start | bytes 393220
  4.1 19.5 %copy-start = (bf16[32,64,128]{2,1,0:T(8,128)(2,1)S(1)}, bf16[32,64,128]{2,1,0:T(8,128)(2,1)}, u32[]{:S(2)}) copy-start(bf16[32,64,128]{2,1,0:T(8,128)(2,1)} %param.17) | copy-start | bytes 1572868
  4.1 19.5 %copy-start.1 = (bf16[32,64,128]{2,1,0:T(8,128)(2,1)S(1)}, bf16[32,64,128]{2,1,0:T(8,128)(2,1)}, u32[]{:S(2)}) copy-start(bf16[32,64,128]{2,1,0:T(8,128)(2,1)} %param.21) | copy-start | bytes 1572868
  4.4 19.2 %copy-start.2 = (bf16[1024,128]{1,0:T(8,128)(2,1)S(1)}, bf16[1024,128]{1,0:T(8,128)(2,1)}, u32[]{:S(2)}) copy-start(bf16[1024,128]{1,0:T(8,128)(2,1)} %map_ref.1) | copy-start | bytes 786436
  23.5 0.7 copy-start.5
  23.6 0.7 copy-start.6

commit v3 on v2

--- a/solution.py
+++ b/solution.py
@@ -16,24 +16,6 @@
 MESH = pl.DeviceIdType.MESH
 VM = pl.BlockSpec(memory_space=pltpu.VMEM)
 LANES = 128
-
-
-def standardize_features(values, gain_vec):
-    average = jnp.mean(values, axis=-1, keepdims=True)
-    centred = values - average
-    variance = jnp.mean(centred * centred, axis=-1, keepdims=True)
-    inv_scale = lax.rsqrt(variance + EPSILON)
-    vhat_values = centred * inv_scale
-    return (vhat_values * gain_vec, vhat_values, inv_scale)
-
-
-def standardize_reverse_mode(incoming, vhat_values, inv_scale, gain_vec):
-    scaled = incoming * gain_vec
-    return inv_scale * (
-        scaled
-        - jnp.mean(scaled, axis=-1, keepdims=True)
-        - vhat_values * jnp.mean(scaled * vhat_values, axis=-1, keepdims=True)
-    )
 
 
 def positions(rows, cols):
@@ -168,133 +150,20 @@
     )(left, right)
 
 
-def scatter_kernel(
-    rows, cols, left_ref, right_ref, weight_ref, left_out, right_out, weight_out,
-    right_got, weight_got, right_sum,
-    own_sem, hop_send, hop_recv, left_send, left_recv, right_send, right_recv,
-    weight_send, weight_recv,
+def reduce_kernel(
+    rows, cols, channels, fold, left_ref, right_ref, weight_ref, hat_ref, inv_ref, gain_ref, fac_ref,
+    align_ref, big_out, small_out,
+    left_got, right_got, weight_got, right_sum, right_mine, right_f, big_mine, big_got,
+    small_f, small_mine, small_got, small_col,
+    hop_send, hop_recv, left_send, left_recv, right_send, right_recv, weight_send, weight_recv,
+    big_send, big_recv, small_send, small_recv, bigc_send, bigc_recv, smallc_send, smallc_recv,
+    bigr_send, bigr_recv, smallr_send, smallr_recv,
 ):
     r, z, here, there = positions(rows, cols)
     apart = here != there
     to = (there // cols, lax.rem(there, cols))
     source = (lax.rem(here, rows), here // rows)
     greet(rows, cols, r, z, (to, source), apart)
-
-    started = []
-    for k in range(1, rows):
-        peer = lax.rem(r + k, rows)
-        copy = send(
-            right_ref.at[peer], right_got.at[r], right_send.at[k], right_recv.at[k], (peer, z)
-        )
-        copy.start()
-        started.append(copy)
-    for k in range(1, cols):
-        peer = lax.rem(z + k, cols)
-        copy = send(
-            left_ref.at[peer], left_out.at[z], left_send.at[k], left_recv.at[k], (r, peer)
-        )
-        copy.start()
-        started.append(copy)
-    for k in range(1, rows):
-        peer = lax.rem(r + k, rows)
-        copy = send(
-            weight_ref.at[peer], weight_got.at[r], weight_send.at[k], weight_recv.at[k], (peer, z)
-        )
-        copy.start()
-        started.append(copy)
-    own = pltpu.make_async_copy(left_ref.at[z], left_out.at[z], own_sem)
-    own.start()
-
-    for k in range(1, rows):
-        origin = lax.rem(r - k + rows, rows)
-        send(
-            right_ref.at[r], right_got.at[origin], right_send.at[k], right_recv.at[k], (origin, z)
-        ).wait_recv()
-    total = right_ref[r].astype(F32)
-    for k in range(1, rows):
-        total = total + right_got[lax.rem(r - k + rows, rows)].astype(F32)
-    right_sum[...] = total.astype(BF16)
-
-    hop = send(right_sum, right_out, hop_send, hop_recv, to)
-    stay = pltpu.make_async_copy(right_sum, right_out, hop_send)
-
-    @pl.when(apart)
-    def _():
-        hop.start()
-
-    @pl.when(jnp.logical_not(apart))
-    def _():
-        stay.start()
-
-    for k in range(1, rows):
-        origin = lax.rem(r - k + rows, rows)
-        send(
-            weight_ref.at[r], weight_got.at[origin], weight_send.at[k], weight_recv.at[k],
-            (origin, z),
-        ).wait_recv()
-    total = weight_ref[r].astype(F32)
-    for k in range(1, rows):
-        total = total + weight_got[lax.rem(r - k + rows, rows)].astype(F32)
-    weight_out[...] = total.astype(BF16)
-
-    own.wait()
-    for k in range(1, cols):
-        origin = lax.rem(z - k + cols, cols)
-        send(
-            left_ref.at[z], left_out.at[origin], left_send.at[k], left_recv.at[k], (r, origin)
-        ).wait_recv()
-
-    @pl.when(apart)
-    def _():
-        hop.wait()
-
-    @pl.when(jnp.logical_not(apart))
-    def _():
-        stay.wait()
-
-    for copy in started:
-        copy.wait_send()
-
-
-def scatter_grads(rows, cols, left, right, weight):
-    return pl.pallas_call(
-        functools.partial(scatter_kernel, rows, cols),
-        out_shape=(
-            jax.ShapeDtypeStruct(left.shape, left.dtype),
-            jax.ShapeDtypeStruct(right.shape[1:], right.dtype),
-            jax.ShapeDtypeStruct(weight.shape[1:], weight.dtype),
-        ),
-        in_specs=[VM] * 3,
-        out_specs=(VM,) * 3,
-        scratch_shapes=[
-            pltpu.VMEM(right.shape, right.dtype),
-            pltpu.VMEM(weight.shape, weight.dtype),
-            pltpu.VMEM(right.shape[1:], right.dtype),
-            pltpu.SemaphoreType.DMA(()),
-            pltpu.SemaphoreType.DMA(()),
-            pltpu.SemaphoreType.DMA(()),
-            pltpu.SemaphoreType.DMA((cols,)),
-            pltpu.SemaphoreType.DMA((cols,)),
-            pltpu.SemaphoreType.DMA((rows,)),
-            pltpu.SemaphoreType.DMA((rows,)),
-            pltpu.SemaphoreType.DMA((rows,)),
-            pltpu.SemaphoreType.DMA((rows,)),
-        ],
-        compiler_params=pltpu.CompilerParams(
-            collective_id=1, has_side_effects=True, vmem_limit_bytes=24 << 20
-        ),
-    )(left, right, weight)
-
-
-def total_kernel(
-    rows, cols, big_ref, small_ref, big_out, small_out,
-    big_got, small_got, small_col,
-    big_send, big_recv, small_send, small_recv,
-    bigc_send, bigc_recv, smallc_send, smallc_recv,
-    bigr_send, bigr_recv, smallr_send, smallr_recv,
-):
-    r, z, _, _ = positions(rows, cols)
-    greet(rows, cols, r, z)
     started = []
 
     def go(src, dst, sends, recvs, k, device):
@@ -307,35 +176,112 @@
 
     for k in range(1, rows):
         peer = lax.rem(r + k, rows)
-        go(small_ref.at[peer], small_got.at[r], small_send, small_recv, k, (peer, z))
+        go(right_ref.at[peer], right_got.at[r], right_send, right_recv, k, (peer, z))
+    for k in range(1, rows):
+        peer = lax.rem(r + k, rows)
+        go(weight_ref.at[peer], weight_got.at[r], weight_send, weight_recv, k, (peer, z))
     for k in range(1, cols):
         peer = lax.rem(z + k, cols)
-        go(big_ref.at[peer], big_got.at[z], big_send, big_recv, k, (r, peer))
-
-    total = big_ref[z].astype(F32)
+        go(left_ref.at[peer], left_got.at[z], left_send, left_recv, k, (r, peer))
+
+    total = right_ref[r].astype(F32)
+    for k in range(1, rows):
+        origin = lax.rem(r - k + rows, rows)
+        arrive(right_ref.at[r], right_got.at[origin], right_send, right_recv, k, (origin, z))
+        total = total + right_got[origin].astype(F32)
+    right_sum[...] = total.astype(BF16)
+    hop = send(right_sum, right_mine, hop_send, hop_recv, to)
+    stay = pltpu.make_async_copy(right_sum, right_mine, hop_send)
+
+    @pl.when(apart)
+    def _():
+        hop.start()
+
+    @pl.when(jnp.logical_not(apart))
+    def _():
+        stay.start()
+
+    total = weight_ref[r].astype(F32)
+    for k in range(1, rows):
+        origin = lax.rem(r - k + rows, rows)
+        arrive(weight_ref.at[r], weight_got.at[origin], weight_send, weight_recv, k, (origin, z))
+        total = total + weight_got[origin].astype(F32)
+    big_mine[...] = total.reshape(big_mine.shape).astype(BF16)
+    for k in range(1, cols):
+        peer = lax.rem(z + k, cols)
+        go(big_mine.at[peer], big_got.at[z], big_send, big_recv, k, (r, peer))
+
+    left_sum = left_ref[z].astype(F32)
     for k in range(1, cols):
         origin = lax.rem(z - k + cols, cols)
-        arrive(big_ref.at[z], big_got.at[origin], big_send, big_recv, k, (r, origin))
+        arrive(left_ref.at[z], left_got.at[origin], left_send, left_recv, k, (r, origin))
+        left_sum = left_sum + left_got[origin].astype(F32)
+    left_sum = left_sum.astype(BF16)
+
+    total = big_mine[z].astype(F32)
+    for k in range(1, cols):
+        origin = lax.rem(z - k + cols, cols)
+        arrive(big_mine.at[z], big_got.at[origin], big_send, big_recv, k, (r, origin))
         total = total + big_got[origin].astype(F32)
     big_out[r, z] = total.astype(BF16)
     for k in range(1, cols):
         go(big_out.at[r, z], big_out.at[r, z], bigc_send, bigc_recv, k, (r, lax.rem(z + k, cols)))
 
-    total = small_ref[r].astype(F32)
+    @pl.when(apart)
+    def _():
+        hop.wait()
+
+    @pl.when(jnp.logical_not(apart))
+    def _():
+        stay.wait()
+
+    shard, features, seqs = hat_ref.shape
+    right_f[...] = right_mine[...].astype(F32)
+    gain = jnp.broadcast_to(gain_ref[...], (seqs, features)).T
+    factors = jnp.zeros((2 * channels, features), F32)
+    for at in range(shard):
+        p, f = at // fold, at % fold
+        side = jnp.concatenate(
+            [
+                left_sum[p * channels : (p + 1) * channels, f * seqs : (f + 1) * seqs],
+                right_f[pl.ds(at, channels, stride=shard), :].astype(BF16),
+            ],
+            axis=0,
+        )
+        hat = hat_ref[at]
+        scaled = mm(fac_ref[...], side) * gain
+        align_ref[at] = (
+            inv_ref[at]
+            * (
+                scaled
+                - jnp.mean(scaled, axis=0, keepdims=True)
+                - hat * jnp.mean(scaled * hat, axis=0, keepdims=True)
+            )
+        ).astype(BF16)
+        factors = factors + mm_t(side, (hat * gain).astype(BF16))
+    width = small_f.shape[1]
+    small_f[...] = jnp.zeros_like(small_f)
+    for h in range(features // width):
+        small_f[pl.ds(h * 2 * channels, 2 * channels), :] = factors[:, h * width : (h + 1) * width]
+    small_mine[...] = small_f[...].reshape(small_mine.shape).astype(BF16)
+
+    for k in range(1, rows):
+        peer = lax.rem(r + k, rows)
+        go(small_mine.at[peer], small_got.at[r], small_send, small_recv, k, (peer, z))
+    for k in range(1, cols):
+        origin = lax.rem(z - k + cols, cols)
+        arrive(big_out.at[r, z], big_out.at[r, origin], bigc_send, bigc_recv, k, (r, origin))
+    for k in range(1, rows):
+        go(big_out.at[r], big_out.at[r], bigr_send, bigr_recv, k, (lax.rem(r + k, rows), z))
+
+    total = small_mine[r].astype(F32)
     for k in range(1, rows):
         origin = lax.rem(r - k + rows, rows)
-        arrive(small_ref.at[r], small_got.at[origin], small_send, small_recv, k, (origin, z))
+        arrive(small_mine.at[r], small_got.at[origin], small_send, small_recv, k, (origin, z))
         total = total + small_got[origin].astype(F32)
     small_col[z] = total.astype(BF16)
     for k in range(1, cols):
         go(small_col.at[z], small_col.at[z], smallc_send, smallc_recv, k, (r, lax.rem(z + k, cols)))
-
-    for k in range(1, cols):
-        origin = lax.rem(z - k + cols, cols)
-        arrive(big_out.at[r, z], big_out.at[r, origin], bigc_send, bigc_recv, k, (r, origin))
-    for k in range(1, rows):
-        go(big_out.at[r], big_out.at[r], bigr_send, bigr_recv, k, (lax.rem(r + k, rows), z))
-
     for k in range(1, cols):
         origin = lax.rem(z - k + cols, cols)
         arrive(small_col.at[z], small_col.at[origin], smallc_send, smallc_recv, k, (r, origin))
@@ -345,7 +291,6 @@
     small_out[r] = total.astype(BF16)
     for k in range(1, rows):
         go(small_out.at[r], small_out.at[r], smallr_send, smallr_recv, k, (lax.rem(r + k, rows), z))
-
     for k in range(1, rows):
         origin = lax.rem(r - k + rows, rows)
         arrive(big_out.at[r], big_out.at[origin], bigr_send, bigr_recv, k, (origin, z))
@@ -354,27 +299,42 @@
         copy.wait_send()
 
 
-def total_weights(rows, cols, big, small):
+def reduce_grads(rows, cols, channels, fold, each, left, right, weight, hat, inv, gain, factor):
     by_row = [pltpu.SemaphoreType.DMA((rows,))] * 2
     by_col = [pltpu.SemaphoreType.DMA((cols,))] * 2
+    weight_rows, width = weight.shape[1:]
+    part = (cols, weight_rows // cols, width)
+    small = (rows, each, width)
     return pl.pallas_call(
-        functools.partial(total_kernel, rows, cols),
+        functools.partial(reduce_kernel, rows, cols, channels, fold),
         out_shape=(
-            jax.ShapeDtypeStruct((rows,) + big.shape, big.dtype),
-            jax.ShapeDtypeStruct(small.shape, small.dtype),
+            jax.ShapeDtypeStruct(hat.shape, BF16),
+            jax.ShapeDtypeStruct((rows,) + part, BF16),
+            jax.ShapeDtypeStruct(small, BF16),
         ),
-        in_specs=[VM] * 2,
-        out_specs=(VM,) * 2,
+        in_specs=[VM] * 7,
+        out_specs=(VM,) * 3,
         scratch_shapes=[
-            pltpu.VMEM(big.shape, big.dtype),
-            pltpu.VMEM(small.shape, small.dtype),
-            pltpu.VMEM((cols,) + small.shape[1:], small.dtype),
+            pltpu.VMEM(left.shape, BF16),
+            pltpu.VMEM(right.shape, BF16),
+            pltpu.VMEM(weight.shape, BF16),
+            pltpu.VMEM(right.shape[1:], BF16),
+            pltpu.VMEM(right.shape[1:], BF16),
+            pltpu.VMEM(right.shape[1:], F32),
+            pltpu.VMEM(part, BF16),
+            pltpu.VMEM(part, BF16),
+            pltpu.VMEM((rows * each, width), F32),
+            pltpu.VMEM(small, BF16),
+            pltpu.VMEM(small, BF16),
+            pltpu.VMEM((cols,) + small[1:], BF16),
+            pltpu.SemaphoreType.DMA(()),
+            pltpu.SemaphoreType.DMA(()),
         ]
-        + by_col + by_row + by_col + by_col + by_row + by_row,
+        + by_col + by_row + by_row + by_col + by_row + by_col + by_col + by_row + by_row,
         compiler_params=pltpu.CompilerParams(
-            collective_id=2, has_side_effects=True, vmem_limit_bytes=24 << 20
+            collective_id=1, has_side_effects=True, vmem_limit_bytes=24 << 20
         ),
-    )(big, small)
+    )(left, right, weight, hat, inv, gain, factor)
 
 
 def mm(a, b):
@@ -553,14 +513,16 @@
     pairs = row_count * col_count
     cc = channels * channels
 
-    full, msa_hat, msa_inv = standardize_features(
-        alignment_tensor.astype(F32), alignment_scaling_vector
-    )
-    normed = full.astype(BF16)
-    left = jnp.einsum("srm,mc->rcs", normed, first_factor_matrix, preferred_element_type=F32)
+    turned = alignment_tensor.transpose(1, 2, 0).astype(F32)
+    average = jnp.mean(turned, axis=1, keepdims=True)
+    centred = turned - average
+    msa_inv = lax.rsqrt(jnp.mean(centred * centred, axis=1, keepdims=True) + EPSILON)
+    msa_hat = centred * msa_inv
+    normed = (msa_hat * alignment_scaling_vector[None, :, None]).astype(BF16)
+    left = jnp.einsum("rms,mc->rcs", normed, first_factor_matrix, preferred_element_type=F32)
     left = left.astype(BF16).reshape(local_groups, fold, channels, seqs)
     left = left.transpose(0, 2, 1, 3).reshape(local_groups * channels, fold * seqs)
-    right = jnp.einsum("srm,me->ers", normed, second_factor_matrix, preferred_element_type=F32)
+    right = jnp.einsum("rms,me->ers", normed, second_factor_matrix, preferred_element_type=F32)
     right = right.astype(BF16).reshape(channels * shard, seqs)
 
     left_all, right_all = gather_sides(rows, cols, left, right)
@@ -608,36 +570,23 @@
         upstream_sensitivity.reshape(pairs, width),
     )
 
-    left_got, right_grad, big = scatter_grads(
+    small_rows = 2 * channels * features // width
+    each = -(-small_rows // (rows * 16)) * 16
+    aligned, big_all, small_all = reduce_grads(
         rows,
         cols,
+        channels,
+        fold,
+        each,
         left_part.reshape(cols, local_groups * channels, fold * seqs),
         right_part,
         weight_part.reshape(rows, weight_rows // rows, width),
+        msa_hat,
+        msa_inv,
+        alignment_scaling_vector.reshape(1, features),
+        jnp.concatenate([first_factor_matrix, second_factor_matrix], axis=1),
     )
-    left_grad = jnp.sum(left_got.astype(F32), axis=0).astype(BF16)
-    left_grad = left_grad.reshape(local_groups, channels, fold, seqs)
-    left_grad = left_grad.transpose(0, 2, 1, 3).reshape(shard, channels, seqs)
-    right_grad = right_grad.reshape(channels, shard, seqs).transpose(1, 0, 2)
-    both_grad = jnp.concatenate([left_grad, right_grad], axis=1)
-    both_factor = jnp.concatenate([first_factor_matrix, second_factor_matrix], axis=1)
-    both_weight = jnp.einsum("srm,rcs->cm", normed, both_grad, preferred_element_type=F32)
-    incoming = jnp.einsum("rcs,mc->srm", both_grad, both_factor, preferred_element_type=F32)
-    alignment_sensitivity = standardize_reverse_mode(
-        incoming, msa_hat, msa_inv, alignment_scaling_vector
-    ).astype(BF16)
-
-    small_rows = 2 * channels * features // width
-    each = -(-small_rows // (rows * 16)) * 16
-    small = both_weight.astype(BF16).reshape(2 * channels, features // width, width)
-    small = small.transpose(1, 0, 2).reshape(small_rows, width)
-    small = jnp.pad(small, ((0, each * rows - small_rows), (0, 0)))
-    big_all, small_all = total_weights(
-        rows,
-        cols,
-        big.reshape(cols, weight_rows // (rows * cols), width),
-        small.reshape(rows, each, width),
-    )
+    alignment_sensitivity = aligned.transpose(2, 0, 1)
     out_proj, trans_in, trans_out, first, second = pl.pallas_call(
         functools.partial(finish_kernel, 1.0 / amino_number, channels, cc, hid),
         out_shape=(

time: 87.9 us -> 85.2 us (0.969)
  Pallas kernels: 78.7 us -> 76.8 us
    pallas_call x2 -> x1, Pallas kernels: 33.8 us -> 31.9 us  [reduce_grads(): pl.pallas_call(functools.partial(reduce_kernel, rows, cols, channels, fol...]
    unnamed x25 -> x27, local copies, waits for them, and re-layouts: 5.97 us -> 6.21 us
where the time goes in v3:
time: 85.2 us; the launch traced here: 84.9 us
  Pallas kernels  76.8 us (90%)
  local copies, waits for them, and re-layouts  6.29 us (7%)
    pallas_call x1, Pallas kernels, reduce_grads(): pl.pallas_call(functools.partial(reduce_kernel, rows, cols, channels, fol...  31.9 us
    pallas_call x1, Pallas kernels, on_device(): pl.pallas_call(functools.partial(pair_kernel, 1.0 / seqs, channels, col_c...  24.7 us
    pallas_call x1, Pallas kernels, gather_sides(): pl.pallas_call(functools.partial(gather_kernel, rows, cols), out_shape=(j...  19.1 us
    unnamed x27, local copies, waits for them, and re-layouts  6.21 us

profile of v3, /device:TPU:0, one launch (start us, length us, event | category | flops | bytes accessed | tf_op | source)
XLA Modules:
  0.0 84.9 jit_solution(15722989903242455335)
XLA Ops:
  0.6 1.5 %copy.19 = bf16[128,8,256]{0,2,1:T(8,128)(2,1)S(1)} copy(bf16[128,8,256]{2,1,0:T(8,128)(2,1)} %param.11) | data formatting | bytes 1048576 | tf_op args[0]
  2.1 0.1 bitcast_reduce_fusion
  2.2 0.0 copy-start.9
  2.2 0.1 fusion.3
  2.4 0.0 copy-start.5
  2.4 0.5 copy-done.9
  2.9 0.1 copy-done.5
  3.1 0.3 convolution_convert_fusion.1
  3.3 0.0 copy-start.8
  3.4 0.0 copy-start.4
  3.4 0.1 copy.20
  3.4 0.0 copy-start.3
  3.5 0.6 copy-done.8
  4.1 0.0 copy-start
  4.1 0.0 copy-start.1
  4.1 0.3 fusion
  4.4 0.0 copy-start.2
  4.4 19.1 %shard_map.170 = (bf16[4,128,256]{2,1,0:T(8,128)(2,1)S(1)}, bf16[8,256,128]{2,1,0:T(8,128)(2,1)S(1)}) custom-call(bf16[128,256]{1,0:T(8,128)(2,1)S(1)} %bitcast.54, bf16[256,128]{1,0:T(8,128)(2,1)S(1)} %bitcast.55), custom_call_target="tpu_custom_call" | custom-call | tf_op jit(solution)/shard_map/pallas_call | solution.py:130
  23.5 0.0 copy-start.6
  23.6 0.0 copy-start.7
  23.6 0.0 copy-done.4
  23.6 0.0 copy-done.3
  23.6 0.0 copy-done
  23.6 0.0 copy-done.1
  23.6 0.0 copy-done.2
  23.6 0.6 copy-done.6
  24.2 0.0 copy-done.7
  24.2 24.7 %shard_map.171 = (bf16[2048,128]{1,0:T(8,128)(2,1)}, bf16[2048,128]{1,0:T(8,128)(2,1)}, bf16[512,256]{1,0:T(8,128)(2,1)S(1)}, bf16[8,256,128]{2,1,0:T(8,128)(2,1)S(1)}, bf16[2048,128]{1,0:T(8,128)(2,1)S(1)}) custom-call(bf16[512,256]{1,0:T(8,128)(2,1)S(1)} %bitcast.53, bf16[8,256,128]{2,1,0:T(8,128)(2,1)S(1)} %get-tuple-element.24.r_ref, ...), custom_call_target="tpu_custom_call" | custom-call | tf_op jit(solution)/shard_map/pallas_call | solution.py:554
  48.9 0.1 fusion.1.hat_ref
  49.0 0.1 copy.23
  49.1 0.1 copy.22
  49.3 0.1 pad_maximum_fusion.fac_ref
  49.4 31.9 %shard_map.172 = (bf16[8,256,128]{2,1,0:T(8,128)(2,1)S(1)}, bf16[8,4,64,128]{3,2,1,0:T(8,128)(2,1)S(1)}, bf16[8,16,128]{2,1,0:T(8,128)(2,1)S(1)}) custom-call(bf16[4,128,256]{2,1,0:T(8,128)(2,1)S(1)} %bitcast.52, bf16[8,256,128]{2,1,0:T(8,128)(2,1)S(1)} %get-tuple-element.28.right_ref, bf16[8,256,128]{2,1,0:T(8,128)(2,1)S(1)} %bitcast.51, ...), custom_call_target="tpu_custom_call" | custom-call | tf_op jit(solution)/shard_map/pallas_call | solution.py:308
  81.2 1.2 %copy.24 = bf16[128,8,256]{2,1,0:T(8,128)(2,1)} copy(bf16[128,8,256]{0,2,1:T(8,128)(2,1)S(1)} %bitcast.48) | data formatting | bytes 1048576
  82.4 1.1 %shard_map.173 = (f32[1024,128]{1,0:T(8,128)}, f32[128,512]{1,0:T(8,128)}, f32[512,128]{1,0:T(8,128)}, f32[256,32]{1,0:T(8,128)S(1)}, f32[256,32]{1,0:T(8,128)S(1)}) custom-call(bf16[2048,128]{1,0:T(8,128)(2,1)S(1)} %bitcast.47, bf16[128,128]{1,0:T(8,128)(2,1)S(1)} %bitcast.57), custom_call_target="tpu_custom_call" | custom-call | tf_op jit(solution)/shard_map/pallas_call | solution.py:590
  83.5 0.7 copy.25
  84.2 0.7 copy.26
  (4 shorter events, 0.0 us)
Async XLA Ops:
  2.2 0.7 copy-start.9
  2.4 0.7 copy-start.5
  3.3 0.7 copy-start.8
  3.4 20.2 %copy-start.4 = (bf16[512,128]{1,0:T(8,128)(2,1)S(1)}, bf16[512,128]{1,0:T(8,128)(2,1)}, u32[]{:S(2)}) copy-start(bf16[512,128]{1,0:T(8,128)(2,1)} %co_ref.1) | copy-start | bytes 393220
  3.4 20.2 %copy-start.3 = (bf16[128,512]{1,0:T(8,128)(2,1)S(1)}, bf16[128,512]{1,0:T(8,128)(2,1)}, u32[]{:S(2)}) copy-start(bf16[128,512]{1,0:T(8,128)(2,1)} %ex_ref.1) | copy-start | bytes 393220
  4.1 19.5 %copy-start = (bf16[32,64,128]{2,1,0:T(8,128)(2,1)S(1)}, bf16[32,64,128]{2,1,0:T(8,128)(2,1)}, u32[]{:S(2)}) copy-start(bf16[32,64,128]{2,1,0:T(8,128)(2,1)} %param.17) | copy-start | bytes 1572868
  4.1 19.5 %copy-start.1 = (bf16[32,64,128]{2,1,0:T(8,128)(2,1)S(1)}, bf16[32,64,128]{2,1,0:T(8,128)(2,1)}, u32[]{:S(2)}) copy-start(bf16[32,64,128]{2,1,0:T(8,128)(2,1)} %param.21) | copy-start | bytes 1572868
  4.4 19.2 %copy-start.2 = (bf16[1024,128]{1,0:T(8,128)(2,1)S(1)}, bf16[1024,128]{1,0:T(8,128)(2,1)}, u32[]{:S(2)}) copy-start(bf16[1024,128]{1,0:T(8,128)(2,1)} %map_ref.1) | copy-start | bytes 786436
  23.5 0.7 copy-start.6
  23.6 0.7 copy-start.7
